TPU v7x, 128 devices: a whole 4x4x4 slice. The times are simulated.
128 devices in a mesh: ctx: 32 (over z_lo, y, x), head: 4 (over z_hi, core).
Axes of the slice: x: 4, y: 4, z: 4 (z_hi: 2, z_lo: 2; z = z_hi * 2 + z_lo), core: 2. Of those that a mesh axis runs over, the one named last changes fastest.
Arguments:
- main_query: bfloat16 [4096, 73728], P('ctx', 'head'), as said below
- latents: bfloat16 [2048, 576], P('ctx'), may hold values from -6 to 6, as said below
- idx_query: bfloat16 [4096, 8192], P('ctx'), as said below
- idx_weight: float32 [4096, 64], P('ctx'), may hold values from -9 to 9
- idx_keys: bfloat16 [2048, 128], P('ctx'), may hold values from -6 to 6, as said below
- kl_cotangent: float32 [4096], P('ctx'), may hold values from 4 to 64
- query_start: int32 [1], replicated, may hold values from 1024 to 2047
- key_start: int32 [1], replicated, may hold values from 0 to 1023
Outputs:
- grad_query: float32 [4096, 8192], P('ctx', 'head')
- grad_weight: float32 [4096, 64], P('ctx', 'head')
- grad_keys: float32 [2048, 128], P(('ctx', 'head'))
Inputs may be any that keep to these rules, and one draw needn't show every extreme that they name: `latents`: saved latent keys of order one. `idx_keys`: indexer keys of order one. `main_query`: attention queries; a few rows may be large. `idx_query`: indexer queries; a few rows may be large.
All inputs are finite; a program needn't handle non-finite values.
Results may differ from a plain program's by a relative error of at most 0.02.
Values may be sent and summed in bfloat16 or wider, within the bound.
No kernel may reach another device: no remote copies, remote signals or barrier semaphores. Data moves between devices by JAX's collectives and lax.ppermute only.
A program may use at most 128 MiB of HBM per device.

v0:
```python
import jax
import jax.numpy as jnp
from jax import lax
from jax.sharding import Mesh
from jax.sharding import PartitionSpec as P

CTX = ("ctx_0", "ctx_1", "ctx_2")
CTX_HEAD = ("ctx_0", "ctx_1", "ctx_2", "head")


NEGATIVE = -1e30
MAIN_SCALE = 192.0 ** (-0.5)


def in_order(pieces, dim):
    dims = list(pieces.shape[1:])
    dims[dim] *= pieces.shape[0]
    return jnp.moveaxis(pieces, 0, dim).reshape(dims)


def all_blocks(array, axes, sequence):
    pieces = array
    for k in sequence:
        pieces = lax.all_gather(pieces, axes[k])
    done = sequence[::-1]
    back = [done.index(k) for k in range(len(axes))]
    pieces = pieces.transpose(*back, *range(len(axes), pieces.ndim))
    return pieces.reshape(-1, *array.shape)


def gather_axes(array, axes, sequence, dim):
    return in_order(all_blocks(array, axes, sequence), dim)


def cut_along(array, dim, devices):
    dims = array.shape
    pieces = array.reshape(*dims[:dim], devices, dims[dim] // devices, *dims[dim + 1 :])
    return jnp.moveaxis(pieces, dim, 0)


def sum_at_owner(array, axis, dim):
    pieces = cut_along(array, dim, lax.axis_size(axis))
    arrived = lax.all_to_all(pieces, axis, split_axis=0, concat_axis=0, tiled=True)
    return arrived.sum(axis=0)


def sent_to_all(array, axis):
    copies = jnp.broadcast_to(array, (lax.axis_size(axis), *array.shape))
    return lax.all_to_all(copies, axis, split_axis=0, concat_axis=0, tiled=True)


def gathered_once(array, axis):
    leaves = jax.tree.leaves(array)
    sequence = sorted(range(len(leaves)), key=lambda k: -leaves[k].size)
    width = (1, *leaves[sequence[0]].shape)[-1]
    lines = [
        jnp.pad(leaves[k].reshape(-1), (0, -leaves[k].size % width)).reshape(-1, width)
        for k in sequence
    ]
    both, at, found = (sent_to_all(jnp.concatenate(lines), axis), 0, {})
    for k, line in zip(sequence, lines):
        section = both[:, at : at + len(line)].reshape(len(both), -1)
        found[k] = section[:, : leaves[k].size].reshape(-1, *leaves[k].shape)
        at += len(line)
    numbers = iter(range(len(leaves)))
    return jax.tree.map(lambda _: found[next(numbers)], array)


def joined_by_halves(pieces, combine):
    while len(jax.tree.leaves(pieces)[0]) > 1:
        pieces = jax.vmap(combine)(
            *(jax.tree.map(lambda part: part[side::2], pieces) for side in (0, 1))
        )
    return jax.tree.map(lambda part: part[0], pieces)


def joined_all(array, axis, combine):
    pieces = gathered_once(array, axis)
    return joined_by_halves(pieces, combine)


def sum_together(arrays, axis, dims):
    devices = lax.axis_size(axis)
    pieces = [cut_along(a, dim, devices) for a, dim in zip(arrays, dims)]
    lines = jnp.concatenate([b.reshape(devices, -1) for b in pieces], axis=1)
    width = max(16, -(-lines.shape[1] // 1024) * 8)
    lines = jnp.pad(lines, ((0, 0), (0, width * 128 - lines.shape[1]))).reshape(-1, 128)
    flat, at, finished = (lax.psum_scatter(lines, axis, tiled=True).reshape(-1), 0, [])
    for b in pieces:
        part = b[0]
        finished.append(flat[at : at + part.size].reshape(part.shape))
        at += part.size
    return tuple(finished)


def sent_and_summed(array, axis, dim):
    devices = lax.axis_size(axis)
    pieces = lax.all_to_all(cut_along(array, dim, devices), axis, 0, 0, tiled=True)
    return jnp.sum(pieces.astype(jnp.float32), axis=0)


def group_size(heads, per_head, limit):
    group = 1
    while group * 2 <= heads and heads % (group * 2) == 0 and (group * 2 * per_head <= limit):
        group = group * 2
    return group


def head_totals(queries, keys, visible):
    query_rows, heads, width = queries.shape
    key_count = keys.shape[0]
    group = group_size(heads, query_rows, 1024)

    def add_group(group_index, totals):
        block = lax.dynamic_slice_in_dim(queries, group_index * group, group, 1).reshape(
            query_rows * group, width
        )
        scores = lax.dot_general(
            block, keys, (((1,), (1,)), ((), ())), preferred_element_type=jnp.float32
        )
        scores = scores.reshape(query_rows, group, key_count) * MAIN_SCALE
        scores = jnp.where(visible[:, None, :], scores, NEGATIVE)
        largest = jnp.max(scores, axis=-1, keepdims=True)
        weights = jnp.where(visible[:, None, :], jnp.exp(scores - largest), 0.0)
        weights = weights / jnp.sum(weights, axis=-1, keepdims=True)
        return totals + jnp.sum(weights, axis=1)

    start_totals = jnp.zeros((query_rows, key_count), jnp.float32)
    return lax.fori_loop(0, heads // group, add_group, start_totals)


def index_scores(queries, keys, weights):
    query_rows, heads, head_dim = queries.shape
    key_count = keys.shape[0]
    group = group_size(heads, query_rows * key_count, 2**21)
    scale = head_dim ** (-0.5)

    def add_group(group_index, logits):
        block = lax.dynamic_slice_in_dim(queries, group_index * group, group, 1).reshape(
            query_rows * group, head_dim
        )
        inner = lax.dot_general(
            block, keys, (((1,), (1,)), ((), ())), preferred_element_type=jnp.float32
        )
        inner = inner.reshape(query_rows, group, key_count) * scale
        gains = lax.dynamic_slice_in_dim(weights, group_index * group, group, 1)
        return logits + jnp.sum(gains[:, :, None] * jnp.maximum(inner, 0.0), axis=1)

    start_logits = jnp.zeros((query_rows, key_count), jnp.float32)
    return lax.fori_loop(0, heads // group, add_group, start_logits)


def index_grads(queries, keys, weights, upstream):
    query_rows, heads, head_dim = queries.shape
    key_count = keys.shape[0]
    group = group_size(heads, query_rows * key_count, 2**21)
    scale = head_dim ** (-0.5)

    def add_group(group_index, carry):
        query_grad, weight_grad, key_grad = carry
        block = lax.dynamic_slice_in_dim(queries, group_index * group, group, 1).reshape(
            query_rows * group, head_dim
        )
        inner = lax.dot_general(
            block, keys, (((1,), (1,)), ((), ())), preferred_element_type=jnp.float32
        )
        inner = inner.reshape(query_rows, group, key_count) * scale
        gains = lax.dynamic_slice_in_dim(weights, group_index * group, group, 1)
        grad_inner = jnp.where(inner > 0.0, upstream[:, None, :] * gains[:, :, None], 0.0).astype(
            jnp.bfloat16
        )
        part_weight = jnp.sum(upstream[:, None, :] * jnp.maximum(inner, 0.0), axis=-1)
        grad_flat = grad_inner.reshape(query_rows * group, key_count)
        part_query = (
            jnp.dot(grad_flat, keys, preferred_element_type=jnp.float32).reshape(
                query_rows, group, head_dim
            )
            * scale
        )
        part_key = (
            lax.dot_general(
                grad_flat, block, (((0,), (0,)), ((), ())), preferred_element_type=jnp.float32
            )
            * scale
        )
        query_grad = lax.dynamic_update_slice_in_dim(query_grad, part_query, group_index * group, 1)
        weight_grad = lax.dynamic_update_slice_in_dim(
            weight_grad, part_weight, group_index * group, 1
        )
        return (query_grad, weight_grad, key_grad + part_key)

    start_carry = (
        jnp.zeros((query_rows, heads, head_dim), jnp.float32),
        jnp.zeros((query_rows, heads), jnp.float32),
        jnp.zeros((key_count, head_dim), jnp.float32),
    )
    return lax.fori_loop(0, heads // group, add_group, start_carry)


def regroup(values, ctx_count, head_count):
    total_rows = values.shape[0]
    per_block = total_rows // (ctx_count * head_count)
    shaped = values.reshape(ctx_count, head_count, per_block, values.shape[1])
    return shaped.transpose(1, 0, 2, 3).reshape(total_rows, values.shape[1])


def merge_stats(first, second):
    largest = jnp.maximum(first[0], second[0])
    return (
        largest,
        first[1] * jnp.exp(first[0] - largest) + second[1] * jnp.exp(second[0] - largest),
    )


def shards(
    main_query, latents, idx_query, idx_weight, idx_keys, kl_cotangent, query_start, key_start
):
    query_rows = main_query.shape[0]
    width = latents.shape[1]
    heads_here = main_query.shape[1] // width
    idx_heads = idx_weight.shape[1]
    idx_dim = idx_keys.shape[1]
    ctx_count = lax.axis_size(CTX)
    head_count = lax.axis_size("head")
    head_index = lax.axis_index("head")
    slab_latents, slab_index_keys = (
        gather_axes(latents, CTX, (0, 1, 2), 0),
        gather_axes(idx_keys, CTX, (0, 1, 2), 0),
    )
    key_count = slab_latents.shape[0]
    key_order = jnp.arange(key_count, dtype=jnp.int32)[:, None]
    slab_latents = regroup(slab_latents, ctx_count, head_count)
    slab_index_keys = regroup(slab_index_keys, ctx_count, head_count)
    key_order = regroup(key_order, ctx_count, head_count)
    key_position = key_start[0] + key_order[:, 0]
    query_position = (
        query_start[0] + lax.axis_index(CTX) * query_rows + jnp.arange(query_rows, dtype=jnp.int32)
    )
    visible = key_position[None, :] <= query_position[:, None]
    target = head_totals(main_query.reshape(query_rows, heads_here, width), slab_latents, visible)
    all_heads = heads_here * head_count
    block_keys = key_count // head_count
    target_block = sum_at_owner(target, "head", 1) / all_heads
    keys_block = lax.dynamic_slice_in_dim(slab_index_keys, head_index * block_keys, block_keys, 0)
    visible_block = lax.dynamic_slice_in_dim(visible, head_index * block_keys, block_keys, 1)
    queries_index = idx_query.reshape(query_rows, idx_heads, idx_dim)
    logits = index_scores(queries_index, keys_block, idx_weight)
    logits = jnp.where(visible_block, logits, NEGATIVE)
    largest = jnp.max(logits, axis=-1, keepdims=True)
    total_exp = jnp.sum(
        jnp.where(visible_block, jnp.exp(logits - largest), 0.0), axis=-1, keepdims=True
    )
    largest, total_exp = joined_all((largest, total_exp), "head", merge_stats)
    chance = jnp.where(visible_block, jnp.exp(logits - largest) / total_exp, 0.0)
    upstream = kl_cotangent[:, None] * (chance - target_block)
    query_grad, weight_grad, key_grad = index_grads(queries_index, keys_block, idx_weight, upstream)
    grad_query, grad_weight = sum_together(
        (query_grad.reshape(query_rows, idx_heads * idx_dim), weight_grad), "head", (1, 1)
    )
    grad_keys = sent_and_summed(key_grad.astype(jnp.bfloat16), CTX, 0)
    return (grad_query, grad_weight, grad_keys)


def solution(mesh):
    torus = Mesh(
        mesh.devices.reshape(2, 4, 4, mesh.shape["head"]), ("ctx_0", "ctx_1", "ctx_2", "head")
    )
    placed = (
        P(CTX, "head"),
        P(CTX, None),
        P(CTX, None),
        P(CTX, None),
        P(CTX, None),
        P(CTX),
        P(),
        P(),
    )
    return jax.shard_map(
        shards,
        mesh=torus,
        in_specs=placed,
        out_specs=(P(CTX, "head"), P(CTX, "head"), P(CTX_HEAD, None)),
        check_vma=False,
    )
```

profile of v0, /device:TPU:1, one launch (start us, length us, event | category | flops | bytes accessed | tf_op | source)
XLA Modules:
  0.0 377.9 jit_solution(14490168104309544743)
XLA Ops:
  7.2 5.6 %all-gather.3 = bf16[128,576]{1,0:T(8,128)(2,1)S(1)} all-gather(bf16[64,576]{1,0:T(8,128)(2,1)} %param.15), channel_id=5, replica_groups=mesh['ctx_0'=2,'ctx_1'=4,'ctx_2'=4,'head'=4] {'ctx_0'}, dimensions={0}, use_global_device_ids=true | all-gather | bytes 221184 | tf_op jit(solution)/shard_map/all_gather | solution.py:24
  12.8 12.5 %all-gather.4 = bf16[8,64,576]{2,1,0:T(8,128)(2,1)} all-gather(bf16[2,64,576]{2,1,0:T(8,128)(2,1)S(1)} %bitcast.91), channel_id=6, replica_groups=mesh['ctx_0'=2,'ctx_1'=4,'ctx_2'=4,'head'=4] {'ctx_1'}, dimensions={0}, use_global_device_ids=true | all-gather | bytes 737280 | tf_op jit(solution)/shard_map/all_gather | solution.py:24
  25.3 3.5 all-gather
  28.8 9.1 %all-gather.1 = bf16[8,64,128]{2,1,0:T(8,128)(2,1)S(1)} all-gather(bf16[2,64,128]{2,1,0:T(8,128)(2,1)S(1)} %bitcast.95), channel_id=3, replica_groups=mesh['ctx_0'=2,'ctx_1'=4,'ctx_2'=4,'head'=4] {'ctx_1'}, dimensions={0}, use_global_device_ids=true | all-gather | bytes 163840 | tf_op jit(solution)/shard_map/all_gather | solution.py:24
  37.9 13.1 %all-gather.2 = bf16[16,2,64,128]{3,2,1,0:T(8,128)(2,1)S(1)} all-gather(bf16[4,2,64,128]{3,2,1,0:T(8,128)(2,1)S(1)} %bitcast.92), channel_id=4, replica_groups=mesh['ctx_0'=2,'ctx_1'=4,'ctx_2'=4,'head'=4] {'ctx_2'}, dimensions={0}, use_global_device_ids=true | all-gather | bytes 655360 | tf_op jit(solution)/shard_map/all_gather | solution.py:24
  51.1 3.2 copy.54
  54.3 2.9 copy.64
  58.8 5.3 %while.46 = (s32[]{:T(128)}, f32[128,512]{1,0:T(8,128)S(1)}, f32[128,64]{0,1:T(8,128)S(1)}, bf16[128,64,128]{2,0,1:T(8,128)(2,1)}, bf16[512,128]{1,0:T(8,128)(2,...) while((s32[]{:T(128)}, f32[128,512]{1,0:T(8,128)S(1)}, f32[128,64]{0,1:T(8,128)S(1)}, ...), condition=%wide.region_2.0_spmd.clone, body=%wide.region_0.2_spmd.clone.sunk | while | flops 545325056 | bytes 2277533 | solution.py:150
  58.8 2.5 multiply_reduce_fusion.4
  61.5 2.5 multiply_reduce_fusion.4
  65.1 14.6 %all-to-all-start = ((f32[4,256,1]{1,2,0:T(1,128)}), f32[4,256,1]{1,2,0:T(1,128)}, u32[]{:S(2)}, u32[]{:S(2)}) async-start(f32[4,256,1]{1,2,0:T(1,128)} %broadcast_in_dim.89), calls=%async_computation | async-start | bytes 8192 | tf_op jit(solution)/shard_map/all_to_all | solution.py:49
  79.8 6.6 %copy.58 = bf16[128,18432]{0,1:T(8,128)(2,1)} copy(bf16[128,18432]{1,0:T(8,128)(2,1)} %param.14) | data formatting | bytes 9437184 | tf_op args[0]
  86.4 2.0 copy.59
  88.4 1.7 copy.60
  90.1 2.9 copy.61
  93.1 145.7 %while.47 = (s32[]{:T(128)}, f32[128,2048]{1,0:T(8,128)S(1)}, bf16[128,32,576]{0,2,1:T(8,128)(2,1)}, bf16[2048,576]{0,1:T(8,128)(2,1)S(1)}, s32[128]{0:T(128)S(1...) while((s32[]{:T(128)}, f32[128,2048]{1,0:T(8,128)S(1)}, ...), condition=%wide.region_9.10_spmd.clone, body=%wide.region_5.9_spmd.clone.sunk | while | flops 2445812736 | bytes 50471584 | solution.py:129
  93.3 6.9 %fusion.71 = f32[128,8,2048]{2,0,1:T(8,128)} fusion(bf16[2048,576]{0,1:T(8,128)(2,1)S(1)} %get-tuple-element.691, bf16[128,32,576]{0,2,1:T(8,128)(2,1)} %get-tuple-element.690, s32[]{:T(128)S(6)} %select_n.129), kind=kOutput, calls=%fused_computation.16.clone.1 | convolution fusion | flops 2415919104 | bytes 11927556 | tf_op jit(solution)/shard_map/while/body/eval_jaxpr/dot_general | solution.py:118
  101.1 13.0 %fusion.72 = f32[128,8,2048]{2,0,1:T(8,128)} fusion(f32[128,8,2048]{2,0,1:T(8,128)} %fusion.71, pred[128,2048]{1,0:T(8,128)(4,1)} %broadcast_compare_fusion.2), kind=kOutput, calls=%fused_computation.7.clone.1 | output fusion | flops 12589054 | bytes 17039360 | tf_op jit(solution)/shard_map/while/body/eval_jaxpr/div | solution.py:125
  114.1 13.9 %divide_reduce_fusion.2 = f32[128,2048]{1,0:T(8,128)} fusion(f32[128,8,2048]{2,0,1:T(8,128)} %fusion.72, f32[128,8,2048]{2,0,1:T(8,128)} %fusion.71, pred[128,2048]{1,0:T(8,128)(4,1)} %broadcast_compare_fusion.2), kind=kOutput, calls=%fused_computation.11.clone.1 | output fusion | flops 16518143 | bytes 18087936 | tf_op jit(solution)/shard_map/while/body/eval_jaxpr/sub | solution.py:124
  128.1 1.6 select_add_fusion.5
  129.6 6.9 %fusion.71 = f32[128,8,2048]{2,0,1:T(8,128)} fusion(bf16[2048,576]{0,1:T(8,128)(2,1)S(1)} %get-tuple-element.691, bf16[128,32,576]{0,2,1:T(8,128)(2,1)} %get-tuple-element.690, s32[]{:T(128)S(6)} %select_n.129), kind=kOutput, calls=%fused_computation.16.clone.1 | convolution fusion | flops 2415919104 | bytes 11927556 | tf_op jit(solution)/shard_map/while/body/eval_jaxpr/dot_general | solution.py:118
  137.5 13.0 %fusion.72 = f32[128,8,2048]{2,0,1:T(8,128)} fusion(f32[128,8,2048]{2,0,1:T(8,128)} %fusion.71, pred[128,2048]{1,0:T(8,128)(4,1)} %broadcast_compare_fusion.2), kind=kOutput, calls=%fused_computation.7.clone.1 | output fusion | flops 12589054 | bytes 17039360 | tf_op jit(solution)/shard_map/while/body/eval_jaxpr/div | solution.py:125
  150.5 13.9 %divide_reduce_fusion.2 = f32[128,2048]{1,0:T(8,128)} fusion(f32[128,8,2048]{2,0,1:T(8,128)} %fusion.72, f32[128,8,2048]{2,0,1:T(8,128)} %fusion.71, pred[128,2048]{1,0:T(8,128)(4,1)} %broadcast_compare_fusion.2), kind=kOutput, calls=%fused_computation.11.clone.1 | output fusion | flops 16518143 | bytes 18087936 | tf_op jit(solution)/shard_map/while/body/eval_jaxpr/sub | solution.py:124
  164.4 1.6 select_add_fusion.5
  166.0 6.9 %fusion.71 = f32[128,8,2048]{2,0,1:T(8,128)} fusion(bf16[2048,576]{0,1:T(8,128)(2,1)S(1)} %get-tuple-element.691, bf16[128,32,576]{0,2,1:T(8,128)(2,1)} %get-tuple-element.690, s32[]{:T(128)S(6)} %select_n.129), kind=kOutput, calls=%fused_computation.16.clone.1 | convolution fusion | flops 2415919104 | bytes 11927556 | tf_op jit(solution)/shard_map/while/body/eval_jaxpr/dot_general | solution.py:118
  173.9 13.0 %fusion.72 = f32[128,8,2048]{2,0,1:T(8,128)} fusion(f32[128,8,2048]{2,0,1:T(8,128)} %fusion.71, pred[128,2048]{1,0:T(8,128)(4,1)} %broadcast_compare_fusion.2), kind=kOutput, calls=%fused_computation.7.clone.1 | output fusion | flops 12589054 | bytes 17039360 | tf_op jit(solution)/shard_map/while/body/eval_jaxpr/div | solution.py:125
  186.9 13.9 %divide_reduce_fusion.2 = f32[128,2048]{1,0:T(8,128)} fusion(f32[128,8,2048]{2,0,1:T(8,128)} %fusion.72, f32[128,8,2048]{2,0,1:T(8,128)} %fusion.71, pred[128,2048]{1,0:T(8,128)(4,1)} %broadcast_compare_fusion.2), kind=kOutput, calls=%fused_computation.11.clone.1 | output fusion | flops 16518143 | bytes 18087936 | tf_op jit(solution)/shard_map/while/body/eval_jaxpr/sub | solution.py:124
  202.4 6.9 %fusion.71 = f32[128,8,2048]{2,0,1:T(8,128)} fusion(bf16[2048,576]{0,1:T(8,128)(2,1)S(1)} %get-tuple-element.691, bf16[128,32,576]{0,2,1:T(8,128)(2,1)} %get-tuple-element.690, s32[]{:T(128)S(6)} %select_n.129), kind=kOutput, calls=%fused_computation.16.clone.1 | convolution fusion | flops 2415919104 | bytes 11927556 | tf_op jit(solution)/shard_map/while/body/eval_jaxpr/dot_general | solution.py:118
  210.3 13.0 %fusion.72 = f32[128,8,2048]{2,0,1:T(8,128)} fusion(f32[128,8,2048]{2,0,1:T(8,128)} %fusion.71, pred[128,2048]{1,0:T(8,128)(4,1)} %broadcast_compare_fusion.2), kind=kOutput, calls=%fused_computation.7.clone.1 | output fusion | flops 12589054 | bytes 17039360 | tf_op jit(solution)/shard_map/while/body/eval_jaxpr/div | solution.py:125
  223.3 13.9 %divide_reduce_fusion.2 = f32[128,2048]{1,0:T(8,128)} fusion(f32[128,8,2048]{2,0,1:T(8,128)} %fusion.72, f32[128,8,2048]{2,0,1:T(8,128)} %fusion.71, pred[128,2048]{1,0:T(8,128)(4,1)} %broadcast_compare_fusion.2), kind=kOutput, calls=%fused_computation.11.clone.1 | output fusion | flops 16518143 | bytes 18087936 | tf_op jit(solution)/shard_map/while/body/eval_jaxpr/sub | solution.py:124
  240.4 4.8 %all-to-all-start.1 = ((f32[4,128,512]{2,1,0:T(8,128)}), f32[4,128,512]{2,1,0:T(8,128)S(1)}, u32[]{:S(2)}, u32[]{:S(2)}) async-start(f32[4,128,512]{2,1,0:T(8,128)} %copy.63), calls=%async_computation.1 | async-start | bytes 2097152 | tf_op jit(solution)/shard_map/all_to_all | solution.py:43
  246.0 14.4 %all-to-all-done.1 = f32[4,128,512]{2,1,0:T(8,128)S(1)} async-done(((f32[4,128,512]{2,1,0:T(8,128)}), f32[4,128,512]{2,1,0:T(8,128)S(1)}, u32[]{:S(2)}, u32[]{:S(2)}) %all-to-all-start.1) | async-done | bytes 1048608 | tf_op jit(solution)/shard_map/all_to_all | solution.py:43
  261.6 2.5 broadcast_in_dim.84.clone
  264.1 27.4 %while.48 = (s32[]{:T(128)}, f32[128,64,128]{0,2,1:T(8,128)}, f32[128,64]{0,1:T(8,128)S(1)}, f32[512,128]{1,0:T(8,128)S(1)}, bf16[128,64,128]{2,0,1:T(8,128)(2,1...) while((s32[]{:T(128)}, f32[128,64,128]{0,2,1:T(8,128)}, ...), condition=%wide.region_13.14_spmd.clone, body=%wide.region_11.13_spmd.clone.sunk | while | flops 1655304192 | bytes 31834300 | solution.py:197
  264.1 3.0 convert_reduce_fusion.3
  268.4 3.4 fusion.76
  271.7 2.6 fusion.75
  274.3 1.9 copy.77
  277.7 3.0 convert_reduce_fusion.3
  282.0 3.4 fusion.76
  285.4 2.6 fusion.75
  288.0 1.9 copy.77
  291.4 5.4 %copy.66 = f32[4,128,2048]{2,1,0:T(8,128)} copy(f32[4,128,2048]{1,2,0:T(8,128)} %bitcast.79) | data formatting | bytes 8388608 | tf_op jit(solution)/shard_map/transpose | solution.py:38
  296.8 6.8 %copy.75 = f32[1,4,128,2048]{3,1,2,0:T(4,128)} copy(f32[1,4,128,2048]{3,2,1,0:T(8,128)} %bitcast.81) | data formatting | bytes 8388608
  303.9 6.5 %pad_maximum_fusion = f32[4,264192]{1,0:T(4,128)} fusion(f32[4,2048]{1,0:T(4,128)S(1)} %reshape.144, f32[4,262144]{1,0:T(4,128)} %bitcast.80), kind=kLoop, calls=%fused_computation.62 | loop fusion | flops 1056768 | bytes 8454144 | tf_op jit(solution)/shard_map/concatenate | solution.py:85
  310.4 6.3 %reshape.145 = f32[8256,128]{1,0:T(8,128)} reshape(f32[4,264192]{1,0:T(4,128)} %pad_maximum_fusion) | data formatting | bytes 8454144 | tf_op jit(solution)/shard_map/reshape | solution.py:87
  316.8 13.5 %all_to_all.15 = bf16[32,16,128]{2,1,0:T(8,128)(2,1)S(1)} all-to-all(bf16[32,16,128]{2,1,0:T(8,128)(2,1)S(1)} %bitcast.93), channel_id=1, replica_groups=mesh['ctx_0'=2,'ctx_1'=4,'ctx_2'=4,'head'=4] {'ctx_0','ctx_1','ctx_2'}, dimensions={0} | all-to-all | bytes 262144 | tf_op jit(solution)/shard_map/all_to_all | solution.py:98
  330.9 36.3 %reduce-scatter.2.cloned.1.call-done = f32[2064,128]{1,0:T(8,128)} async-done(((f32[8256,128]{1,0:T(8,128)}), f32[2064,128]{1,0:T(8,128)}) %reduce-scatter.2.cloned.1.call-update) | async-done | bytes 1056784 | tf_op jit(solution)/shard_map/reduce_scatter | solution.py:88
  (59 shorter events, 22.4 us)
Async XLA Ops:
  7.2 51.6 %copy-start.1 = (f32[128,64]{0,1:T(8,128)S(1)}, f32[128,64]{0,1:T(8,128)}, u32[]{:S(2)}) copy-start(f32[128,64]{0,1:T(8,128)} %param.17) | copy-start | bytes 98308
  7.2 79.2 %all-gather.8.cloned.1.call-start = ((), (), s32[]{:S(2)}) async-start(), calls=%async_computation.5 | async-start | bytes 3276800 | tf_op jit(solution)/shard_map/all_gather | solution.py:24
  64.1 1.0 copy-start
  65.1 175.3 %all-to-all-start = ((f32[4,256,1]{1,2,0:T(1,128)}), f32[4,256,1]{1,2,0:T(1,128)}, u32[]{:S(2)}, u32[]{:S(2)}) async-start(f32[4,256,1]{1,2,0:T(1,128)} %broadcast_in_dim.89), calls=%async_computation | async-start | bytes 8192 | tf_op jit(solution)/shard_map/all_to_all | solution.py:49
  238.8 25.3 %copy-start.2 = (f32[128,64]{0,1:T(8,128)S(1)}, f32[128,64]{0,1:T(8,128)}, u32[]{:S(2)}) copy-start(f32[128,64]{0,1:T(8,128)} %param.17) | copy-start | bytes 98308
  240.4 19.9 %all-to-all-start.1 = ((f32[4,128,512]{2,1,0:T(8,128)}), f32[4,128,512]{2,1,0:T(8,128)S(1)}, u32[]{:S(2)}, u32[]{:S(2)}) async-start(f32[4,128,512]{2,1,0:T(8,128)} %copy.63), calls=%async_computation.1 | async-start | bytes 2097152 | tf_op jit(solution)/shard_map/all_to_all | solution.py:43
  245.2 122.0 %reduce-scatter.2.cloned.1.call-start = ((), (), s32[]{:S(2)}) async-start(), calls=%async_computation.4 | async-start | bytes 5283840 | tf_op jit(solution)/shard_map/reduce_scatter | solution.py:88
Sparse Core Ops, SparseCore 0:
  25.4 43.2 all-gather.7
  316.9 50.2 reduce-scatter.1
where the time goes:
time: 380 us; the launch traced here: 378 us
  other arithmetic  129 us (34%)
  blocking collectives  57.2 us (15%)
  local copies, waits for them, and re-layouts  54.7 us (14%)
  waiting for transfers between devices  50.7 us (13%)
  matrix products  50.6 us (13%)
  starting transfers between devices  19.5 us (5%)
  between operations  15.5 us (4%)
    sub x4, other arithmetic, add_group(): weights = jnp.where(visible[:, None, :], jnp.exp(scores - largest), 0.0)  55.7 us
    div x4, other arithmetic, add_group(): weights = weights / jnp.sum(weights, axis=-1, keepdims=True)  52 us
    all_gather x5, blocking collectives, all_blocks(): pieces = lax.all_gather(pieces, axes[k])  43.7 us
    dot_general x8, matrix products, add_group(): lax.dot_general(block, keys, (((1,), (1,)), ((), ())), preferred_element_...  38.7 us
    reduce_scatter x1, waiting for transfers between devices, sum_together(): lax.psum_scatter(lines, axis, tiled=True).reshape(-1)  36.3 us
    unnamed x12, local copies, waits for them, and re-layouts  23.2 us
    all_to_all x1, starting transfers between devices, sent_to_all(): return lax.all_to_all(copies, axis, split_axis=0, concat_axis=0, tiled=True)  14.6 us
    all_to_all x1, waiting for transfers between devices, sum_at_owner(): lax.all_to_all(pieces, axis, split_axis=0, concat_axis=0, tiled=True)  14.4 us
  transfers between devices with their start and end apart: 4, of which 2 were waited for; matrix products, arithmetic and copies ran while one was open for 46% of the time, Pallas kernels for 0%

commit v1 on v0

v1 whole, which is shorter than its diff:
```python
import functools
import math

import jax
import jax.numpy as jnp
from jax import lax
from jax.experimental import pallas as pl
from jax.experimental.pallas import tpu as pltpu
from jax.sharding import Mesh
from jax.sharding import PartitionSpec as P

CTX = ("ctx_0", "ctx_1", "ctx_2")
HEAD = ("far", "core")
ALL = CTX + HEAD

MAIN_SCALE = 192.0 ** (-0.5)
LOG2E = math.log2(math.e)
bf16, f32 = jnp.bfloat16, jnp.float32


def key_of(place):
    return ((place >> 5) & 31) * 64 + (place >> 10) * 32 + (place & 31)


def lay_halves(keys, own, other, core, width):
    half = own.shape[0]
    keys[pl.ds(pl.multiple_of(core * half, half), half), 0:width] = own[...]
    keys[pl.ds(pl.multiple_of((1 - core) * half, half), half), 0:width] = other[...]


def head_kernel(where, q_ref, own_ref, other_ref, out_ref, keys, pair, scores, probs, acc):
    rows, width = q_ref.shape[0], own_ref.shape[1]
    n_keys = 2 * own_ref.shape[0]
    pairs = q_ref.shape[1] // (2 * width)
    wide = keys.shape[1] - rows
    lay_halves(keys, own_ref, other_ref, where[0], width)
    keys[:, width:wide] = jnp.zeros((n_keys, wide - width), bf16)
    place = lax.broadcasted_iota(jnp.int32, (n_keys, rows), 0)
    query = lax.broadcasted_iota(jnp.int32, (n_keys, rows), 1)
    keys[:, wide:] = jnp.where(key_of(place) > query + where[1], -1e30, 0.0).astype(bf16)
    pair[:, width:wide] = jnp.zeros((2 * rows, wide - width), bf16)
    row = lax.broadcasted_iota(jnp.int32, (2 * rows, rows), 0)
    lane = lax.broadcasted_iota(jnp.int32, (2 * rows, rows), 1)
    pair[:, wide:] = jnp.where((row & (rows - 1)) == lane, 1.0, 0.0).astype(bf16)
    acc[...] = jnp.zeros(acc.shape, f32)
    scale = MAIN_SCALE * LOG2E
    vec = (8, 2 * rows)
    tall = (n_keys // 8, 8, 2 * rows)

    def step(p, product, exponent, add, shift, recip):
        top = total = jnp.zeros(vec, f32)
        if product:
            both = q_ref[:, pl.ds(pl.multiple_of(p * (2 * width), 128), 2 * width)]
            pair[0:rows, 0:width] = both[:, :width]
            pair[rows:, 0:width] = both[:, width:]
        if add:
            old = (probs[...].astype(f32).reshape(tall) * recip[None]).reshape(n_keys, 2 * rows)
            acc[...] += old[:, :rows] + old[:, rows:]
        if exponent:
            e = jnp.exp2(scores[...].reshape(tall) * scale - shift[None])
            total = jnp.sum(e, axis=0)
            probs[...] = e.reshape(n_keys, 2 * rows).astype(bf16)
        if product:
            new = lax.dot_general(
                keys[...], pair[...], (((1,), (1,)), ((), ())), preferred_element_type=f32
            )
            scores[...] = new
            top = jnp.max(new.reshape(tall), axis=0)
        top = jnp.broadcast_to(jnp.max(top, axis=0, keepdims=True), vec)
        total = jnp.broadcast_to(jnp.sum(total, axis=0, keepdims=True), vec)
        return top * scale, 1.0 / jnp.maximum(total, 1e-30)

    zero = jnp.zeros(vec, f32)
    shift, _ = step(0, True, False, False, zero, zero)
    shift, recip = step(1, True, True, False, shift, zero)
    shift, recip = lax.fori_loop(
        2, pairs, lambda p, c: step(p, True, True, True, *c), (shift, recip)
    )
    _, recip = step(pairs, False, True, True, shift, recip)
    step(pairs, False, False, True, zero, recip)
    out_ref[...] = (acc[...] * where[2]).T.astype(bf16)


def head_totals(where, q, own, other):
    rows = q.shape[0]
    n_keys = 2 * own.shape[0]
    vmem = pl.BlockSpec(memory_space=pltpu.VMEM)

    def body(where, *refs):
        head_kernel((where[0], where[1], jnp.float32(1.0 / 128.0)), *refs)

    return pl.pallas_call(
        body,
        out_shape=jax.ShapeDtypeStruct((rows, n_keys), bf16),
        in_specs=[pl.BlockSpec(memory_space=pltpu.SMEM), vmem, vmem, vmem],
        out_specs=vmem,
        scratch_shapes=[
            pltpu.VMEM((n_keys, 768), bf16),
            pltpu.VMEM((2 * rows, 768), bf16),
            pltpu.VMEM((n_keys, 2 * rows), f32),
            pltpu.VMEM((n_keys, 2 * rows), bf16),
            pltpu.VMEM((n_keys, rows), f32),
        ],
        compiler_params=pltpu.CompilerParams(vmem_limit_bytes=56 * 2**20),
        cost_estimate=pl.CostEstimate(
            flops=2 * 32 * rows * n_keys * 768, bytes_accessed=8 * 2**20, transcendentals=2**23
        ),
        name="head_totals",
    )(where, q, own, other)


IDX_GROUP = 8


def forward_kernel(where, q_ref, w_ref, own_ref, other_ref, kl_ref, mask_ref, chance_ref, keys, block, logits):
    g = pl.program_id(0)
    rows, dim = q_ref.shape[0], keys.shape[1]

    @pl.when(g == 0)
    def _():
        lay_halves(keys, own_ref, other_ref, where[0], dim)
        logits[...] = jnp.zeros(logits.shape, f32)

    for j in range(IDX_GROUP):
        block[j * rows : (j + 1) * rows, :] = q_ref[:, j * dim : (j + 1) * dim]
    inner = lax.dot_general(
        block[...], keys[...], (((1,), (1,)), ((), ())), preferred_element_type=f32
    )
    mask_ref[...] = jnp.where(inner > 0.0, 1.0, 0.0).astype(bf16)
    active = jnp.maximum(inner, 0.0)
    weights = w_ref[0] * (dim ** (-0.5))
    total = logits[...]
    for j in range(IDX_GROUP):
        total += active[j * rows : (j + 1) * rows] * weights[:, j : j + 1]
    logits[...] = total

    @pl.when(g == pl.num_programs(0) - 1)
    def _():
        place = lax.broadcasted_iota(jnp.int32, logits.shape, 1)
        query = lax.broadcasted_iota(jnp.int32, logits.shape, 0) + where[2] * rows
        seen = key_of(place) <= query + where[1]
        values = jnp.where(seen, total, -1e30)
        e = jnp.where(seen, jnp.exp(values - jnp.max(values, axis=1, keepdims=True)), 0.0)
        chance_ref[...] = e * (kl_ref[...] / jnp.sum(e, axis=1, keepdims=True))


def index_forward(where, q, w, own, other, kl):
    rows, dim = kl.shape[0], own.shape[1]
    n_keys = 2 * own.shape[0]
    heads = q.shape[1] // dim
    wide = IDX_GROUP * dim
    return pl.pallas_call(
        forward_kernel,
        grid_spec=pltpu.PrefetchScalarGridSpec(
            num_scalar_prefetch=1,
            grid=(heads // IDX_GROUP,),
            in_specs=[
                pl.BlockSpec((rows, wide), lambda g, where: (where[2], g)),
                pl.BlockSpec((1, rows, IDX_GROUP), lambda g, where: (g, 0, 0)),
                pl.BlockSpec((n_keys // 2, dim), lambda g, where: (0, 0)),
                pl.BlockSpec((n_keys // 2, dim), lambda g, where: (0, 0)),
                pl.BlockSpec((rows, 1), lambda g, where: (0, 0)),
            ],
            out_specs=[
                pl.BlockSpec((IDX_GROUP * rows, n_keys), lambda g, where: (g, 0)),
                pl.BlockSpec((rows, n_keys), lambda g, where: (0, 0)),
            ],
            scratch_shapes=[
                pltpu.VMEM((n_keys, dim), bf16),
                pltpu.VMEM((IDX_GROUP * rows, dim), bf16),
                pltpu.VMEM((rows, n_keys), f32),
            ],
        ),
        out_shape=[
            jax.ShapeDtypeStruct((heads * rows, n_keys), bf16),
            jax.ShapeDtypeStruct((rows, n_keys), f32),
        ],
        compiler_params=pltpu.CompilerParams(vmem_limit_bytes=40 * 2**20),
        cost_estimate=pl.CostEstimate(
            flops=2 * heads * rows * n_keys * 256, bytes_accessed=10 * 2**20, transcendentals=2**16
        ),
        name="index_forward",
    )(where, q, w, own, other, kl)


def backward_kernel(where, parts_ref, chance_ref, kl_ref, mask_ref, q_ref, w_ref, own_ref, other_ref, grad_ref, gk_ref, keys, upstream, block, acc):
    g = pl.program_id(0)
    rows, dim = q_ref.shape[0], keys.shape[1]
    scale = dim ** (-0.5)

    @pl.when(g == 0)
    def _():
        lay_halves(keys, own_ref, other_ref, where[0], dim)
        target = parts_ref[0].astype(f32)
        for h in range(1, parts_ref.shape[0]):
            target += parts_ref[h].astype(f32)
        upstream[...] = (chance_ref[...] - kl_ref[...] * target).astype(bf16)
        acc[...] = jnp.zeros(acc.shape, f32)
        grad_ref[:, :, 2048:] = jnp.zeros((4, rows, 128), bf16)

    up = upstream[...]
    masked = mask_ref[...] * jnp.concatenate([up] * IDX_GROUP, axis=0)
    plain = (
        lax.dot_general(masked, keys[...], (((1,), (0,)), ((), ())), preferred_element_type=f32)
        * scale
    )
    owner, side = g // 2, g % 2
    lane = lax.broadcasted_iota(jnp.int32, (rows, 128), 1)
    sums = jnp.zeros((rows, 128), f32)
    for j in range(IDX_GROUP):
        q = q_ref[:, j * dim : (j + 1) * dim].astype(f32)
        gain = w_ref[0, :, j : j + 1]
        own = plain[j * rows : (j + 1) * rows]
        block[j * rows : (j + 1) * rows, :] = (q * gain).astype(bf16)
        grad_ref[owner, :, pl.ds(pl.multiple_of(side * (IDX_GROUP * dim) + j * dim, dim), dim)] = (
            own * gain
        ).astype(bf16)
        sums = jnp.where(
            lane == side * IDX_GROUP + j, jnp.sum(q * own, axis=1, keepdims=True), sums
        )
    grad_ref[owner, :, 2048:] += sums.astype(bf16)
    acc[...] += lax.dot_general(
        block[...], masked, (((0,), (0,)), ((), ())), preferred_element_type=f32
    )

    @pl.when(g == pl.num_programs(0) - 1)
    def _():
        n_keys = acc.shape[1]
        for t in range(n_keys // 128):
            piece = (acc[:, t * 128 : (t + 1) * 128] * scale).T.astype(bf16)
            for b in range(4):
                place = t * 128 + b * 32
                key = ((place >> 5) & 31) * 64 + (place >> 10) * 32
                gk_ref[key : key + 32, :] = piece[b * 32 : (b + 1) * 32]


def index_backward(where, parts, chance, kl, mask, q, w, own, other):
    rows, dim = kl.shape[0], own.shape[1]
    n_keys = 2 * own.shape[0]
    heads = q.shape[1] // dim
    wide = IDX_GROUP * dim

    def whole(*shape):
        return pl.BlockSpec(shape, lambda g, where: (0,) * len(shape))

    return pl.pallas_call(
        backward_kernel,
        grid_spec=pltpu.PrefetchScalarGridSpec(
            num_scalar_prefetch=1,
            grid=(heads // IDX_GROUP,),
            in_specs=[
                whole(4, rows, n_keys),
                whole(rows, n_keys),
                whole(rows, 1),
                pl.BlockSpec((IDX_GROUP * rows, n_keys), lambda g, where: (g, 0)),
                pl.BlockSpec((rows, wide), lambda g, where: (where[2], g)),
                pl.BlockSpec((1, rows, IDX_GROUP), lambda g, where: (g, 0, 0)),
                whole(n_keys // 2, dim),
                whole(n_keys // 2, dim),
            ],
            out_specs=[whole(4, rows, 2048 + 128), whole(n_keys, dim)],
            scratch_shapes=[
                pltpu.VMEM((n_keys, dim), bf16),
                pltpu.VMEM((rows, n_keys), bf16),
                pltpu.VMEM((IDX_GROUP * rows, dim), bf16),
                pltpu.VMEM((dim, n_keys), f32),
            ],
        ),
        out_shape=[
            jax.ShapeDtypeStruct((4, rows, 2048 + 128), bf16),
            jax.ShapeDtypeStruct((n_keys, dim), bf16),
        ],
        compiler_params=pltpu.CompilerParams(vmem_limit_bytes=40 * 2**20),
        cost_estimate=pl.CostEstimate(
            flops=8 * heads * rows * n_keys * 128, bytes_accessed=10 * 2**20, transcendentals=0
        ),
        name="index_backward",
    )(where, parts, chance, kl, mask, q, w, own, other)


def to_all(piece, axes):
    copies = jnp.broadcast_to(piece, (lax.axis_size(axes), *piece.shape))
    return lax.all_to_all(copies, axes, split_axis=0, concat_axis=0, tiled=True)


def gather_halves(array, core):
    half = array.shape[0] // 2
    mine = to_all(lax.dynamic_slice_in_dim(array, core * half, half, 0), CTX)
    mine = mine.reshape(-1, array.shape[1])
    return mine, lax.ppermute(mine, "core", [(0, 1), (1, 0)])


def shards(
    main_query, latents, idx_query, idx_weight, idx_keys, kl_cotangent, query_start, key_start
):
    rows = main_query.shape[0]
    core = lax.axis_index("core")
    head = lax.axis_index(HEAD)
    heads = lax.axis_size(HEAD)
    few = rows // heads
    offset = query_start[0] + lax.axis_index(CTX) * rows - key_start[0]
    where = jnp.stack([core, offset, head]).astype(jnp.int32)

    own_index, other_index = gather_halves(idx_keys, core)
    latents, _ = lax.optimization_barrier((latents, own_index))
    own, other = gather_halves(latents, core)

    kl = lax.dynamic_slice_in_dim(kl_cotangent, head * few, few, 0)[:, None]
    w = lax.dynamic_slice_in_dim(idx_weight, head * few, few, 0)
    w = w.reshape(few, -1, IDX_GROUP).transpose(1, 0, 2)
    mask, chance = index_forward(where, idx_query, w, own_index, other_index, kl)

    target = head_totals(where, main_query, own, other)
    parts = lax.all_to_all(target.reshape(heads, few, -1), HEAD, 0, 0, tiled=True)
    grad, gk = index_backward(
        where, parts, chance, kl, mask, idx_query, w, own_index, other_index
    )
    pieces = lax.all_to_all(gk.reshape(lax.axis_size(ALL), -1, gk.shape[1]), ALL, 0, 0, tiled=True)
    grad_keys = jnp.sum(pieces.astype(f32), axis=0)
    grad = lax.all_to_all(grad, HEAD, 0, 0, tiled=True).reshape(rows, -1).astype(f32)
    return grad[:, :2048], grad[:, 2048 : 2048 + 16], grad_keys


def solution(mesh):
    torus = Mesh(mesh.devices.reshape(2, 4, 4, 2, 2), ALL)
    placed = (
        P(CTX, HEAD),
        P(CTX, None),
        P(CTX, None),
        P(CTX, None),
        P(CTX, None),
        P(CTX),
        P(),
        P(),
    )
    return jax.shard_map(
        shards,
        mesh=torus,
        in_specs=placed,
        out_specs=(P(CTX, HEAD), P(CTX, HEAD), P(ALL, None)),
        check_vma=False,
    )
```

time: 380 us -> 134 us (0.35)
  other arithmetic: 129 us -> 1.5 us
  matrix products: 50.6 us -> 0 us
  local copies, waits for them, and re-layouts: 54.7 us -> 15.1 us
  waiting for transfers between devices: 50.7 us -> 12.5 us
  Pallas kernels: 0 us -> 36.6 us
  between operations: 15.5 us -> 2.05 us
  starting transfers between devices: 19.5 us -> 12.8 us
  blocking collectives: 57.2 us -> 52.8 us
    sub x5 -> x0, other arithmetic: 55.7 us -> none  [the longest x4 55.7 us: add_group(): weights = jnp.where(visible[:, None, :], jnp.exp(scores - largest), 0.0)]
    div x4 -> x0, other arithmetic: 52 us -> none  [add_group(): weights = weights / jnp.sum(weights, axis=-1, keepdims=True)]
    dot_general x12 -> x0, matrix products: 50.6 us -> none  [the longest x8 38.7 us: add_group(): lax.dot_general(block, keys, (((1,), (1,)), ((), ())), preferred_element_...]
    all_gather x5 -> x0, blocking collectives: 43.7 us -> none  [all_blocks(): pieces = lax.all_gather(pieces, axes[k])]
    all_to_all x1 -> x3, blocking collectives: 13.5 us -> 52.8 us  [the longest x2 38.1 us: to_all(): return lax.all_to_all(copies, axes, split_axis=0, concat_axis=0, tiled=True)]
    pallas_call x0 -> x3, Pallas kernels: none -> 36.6 us  [the longest x1 24.2 us: head_totals(): pl.pallas_call(body, out_shape=jax.ShapeDtypeStruct((rows, n_keys), bf16)...]
    reduce_scatter x1 -> x0, waiting for transfers between devices: 36.3 us -> none  [sum_together(): lax.psum_scatter(lines, axis, tiled=True).reshape(-1)]
    unnamed x12 -> x21, local copies, waits for them, and re-layouts: 23.2 us -> 8.94 us
  transfers between devices with their start and end apart: 4 -> 4, of which waited for: 2 -> 2; matrix products, arithmetic and copies ran while one was open for 46% -> 4% of each run, Pallas kernels for 0% -> 22%
where the time goes in v1:
time: 134 us; the launch traced here: 133 us
  blocking collectives  52.8 us (39%)
  Pallas kernels  36.6 us (27%)
  local copies, waits for them, and re-layouts  15.1 us (11%)
  starting transfers between devices  12.8 us (10%)
  waiting for transfers between devices  12.5 us (9%)
  between operations  2.05 us (2%)
  other arithmetic  1.5 us (1%)
    all_to_all x2, blocking collectives, to_all(): return lax.all_to_all(copies, axes, split_axis=0, concat_axis=0, tiled=True)  38.1 us
    pallas_call x1, Pallas kernels, head_totals(): pl.pallas_call(body, out_shape=jax.ShapeDtypeStruct((rows, n_keys), bf16)...  24.2 us
    all_to_all x1, blocking collectives, shards(): lax.all_to_all(grad, HEAD, 0, 0, tiled=True).reshape(rows, -1).astype(f32)  14.7 us
    all_to_all x1, waiting for transfers between devices, shards(): lax.all_to_all(gk.reshape(lax.axis_size(ALL), -1, gk.shape[1]), ALL, 0, 0...  11.7 us
    unnamed x21, local copies, waits for them, and re-layouts  8.94 us
    pallas_call x1, Pallas kernels, index_backward(): pl.pallas_call(backward_kernel, grid_spec=pltpu.PrefetchScalarGridSpec(nu...  6.81 us
    pallas_call x1, Pallas kernels, index_forward(): pl.pallas_call(forward_kernel, grid_spec=pltpu.PrefetchScalarGridSpec(num...  5.55 us
    all_to_all x1, starting transfers between devices, shards(): lax.all_to_all(target.reshape(heads, few, -1), HEAD, 0, 0, tiled=True)  5.23 us
  transfers between devices with their start and end apart: 4, of which 2 were waited for; matrix products, arithmetic and copies ran while one was open for 4% of the time, Pallas kernels for 22%

profile of v1, /device:TPU:1, one launch (start us, length us, event | category | flops | bytes accessed | tf_op | source)
XLA Modules:
  0.0 133.4 jit_solution(15525681546430655164)
XLA Ops:
  0.6 0.0 copy-start
  0.7 0.7 constant_dynamic-slice_fusion.1
  1.4 16.9 %all_to_all.25 = bf16[32,32,128]{2,1,0:T(8,128)(2,1)S(1)} all-to-all(bf16[32,32,128]{2,1,0:T(8,128)(2,1)S(1)} %broadcast_in_dim.9), channel_id=1, replica_groups=mesh['ctx_0'=2,'ctx_1'=4,'ctx_2'=4,'far'=2,'core'=2] {'ctx_0','ctx_1','c..., dimensions={0} | all-to-all | bytes 524288 | tf_op jit(solution)/shard_map/all_to_all | solution.py:283
  18.3 0.0 copy-done
  18.3 0.1 broadcast_in_dim.10
  18.4 21.2 %all_to_all.26 = bf16[32,32,576]{2,1,0:T(8,128)(2,1)S(1)} all-to-all(bf16[32,32,576]{2,1,0:T(8,128)(2,1)S(1)} %broadcast_in_dim.10), channel_id=1, replica_groups=mesh['ctx_0'=2,'ctx_1'=4,'ctx_2'=4,'far'=2,'core'=2] {'ctx_0','ctx_1','c..., dimensions={0} | all-to-all | bytes 2359296 | tf_op jit(solution)/shard_map/all_to_all | solution.py:283
  39.6 0.0 copy-start.7
  39.6 1.5 %copy.18 = bf16[1024,576]{0,1:T(8,128)(2,1)} copy(bf16[1024,576]{1,0:T(8,128)(2,1)S(1)} %bitcast.24) | data formatting | bytes 2359296 | tf_op jit(solution)/shard_map/reshape | solution.py:289
  41.1 3.6 %collective-permute-start = (bf16[1024,576]{0,1:T(8,128)(2,1)}, bf16[1024,576]{0,1:T(8,128)(2,1)}, u32[]{:S(2)}, u32[]{:S(2)}) collective-permute-start(bf16[1024,576]{0,1:T(8,128)(2,1)} %copy.18), channel_id=1, source_target_pairs={{0,1},{1,0},{2,3},{3,2},{4,5},{5,4},{6,7},{7,6},{8,9},{9,8},{10,11... | collective-permute-start | bytes 3538952 | tf_op jit(solution)/shard_map/ppermute | solution.py:290
  46.1 0.7 pad_add_fusion.where
  46.7 0.0 collective-permute-start.1
  46.7 0.9 collective-permute-done
  47.6 0.0 copy-done.7
  47.6 2.4 %copy.19.refs_2_ = bf16[1024,576]{1,0:T(8,128)(2,1)} copy(bf16[1024,576]{0,1:T(8,128)(2,1)} %collective-permute-done) | data formatting | bytes 2359296 | tf_op jit(solution)/shard_map/ppermute | solution.py:290
  50.0 0.0 copy-start.9
  50.0 0.0 copy-start.8
  50.0 0.0 copy-start.1
  50.0 0.0 copy-start.2
  50.0 24.2 %head_totals.1 = bf16[128,2048]{1,0:T(8,128)(2,1)} custom-call(s32[3]{0:T(128)} %pad_add_fusion.where, bf16[128,18432]{1,0:T(8,128)(2,1)} %refs_0_.1, bf16[1024,576]{1,0:T(8,128)(2,1)} %bitcast.25, bf16[1024,576]{1,0:T(8,128)(2,1)} %copy.19.refs_2_), custom_call_target="tpu_custom_call" | custom-call | flops 12884901888 | bytes 8388608 | tf_op jit(solution)/shard_map/head_totals/pallas_call | solution.py:92
  74.2 5.2 %all-to-all-start.2 = ((bf16[4,32,2048]{2,1,0:T(8,128)(2,1)}), bf16[4,32,2048]{2,1,0:T(8,128)(2,1)S(1)}, u32[]{:S(2)}, u32[]{:S(2)}) async-start(bf16[4,32,2048]{2,1,0:T(8,128)(2,1)} %bitcast.26), calls=%async_computation.2 | async-start | bytes 1048576 | tf_op jit(solution)/shard_map/all_to_all | solution.py:314
  79.5 0.0 copy-done.9
  79.5 0.1 dynamic-slice_bitcast_fusion.1
  79.5 0.1 copy.21.kl_ref
  79.6 0.0 copy-done.8
  79.6 0.1 dynamic-slice_bitcast_fusion
  79.7 0.1 copy.20
  79.8 0.0 collective-permute-done.1.other_ref
  79.8 0.0 copy-done.1
  79.8 0.0 copy-done.2
  79.8 5.5 %index_forward.1 = (bf16[2048,2048]{1,0:T(8,128)(2,1)S(1)}, f32[32,2048]{1,0:T(8,128)S(1)}) custom-call(s32[3]{0:T(128)S(1)} %copy-done.1, bf16[128,8192]{1,0:T(8,128)(2,1)S(1)} %copy-done.2, f32[8,32,8]{2,1,0:T(8,128)S(1)} %bitcast.22, bf16[1024,128]{1,0:T(8,128)(2,1)S(1)} %bitcast.20, bf16[1024,128]{1,0:T(8,128)(2,1)S(1)} %collective-permute-done.1.other_ref, ...), custom_call_target="tpu_custom_call" | custom-call | flops 2147483648 | bytes 10485760 | tf_op jit(solution)/shard_map/index_forward/pallas_call | solution.py:152
  85.4 0.0 copy-start.3
  85.4 3.2 %copy-done.3 = bf16[2048,2048]{1,0:T(8,128)(2,1)} copy-done((bf16[2048,2048]{1,0:T(8,128)(2,1)}, bf16[2048,2048]{1,0:T(8,128)(2,1)S(1)}, u32[]{:S(2)}) %copy-start.3) | copy-done | bytes 8388632
  88.6 0.0 copy-start.5
  88.6 0.7 copy-done.5
  89.3 0.0 all-to-all-done.2.parts_ref
  89.3 0.0 copy-start.4
  89.3 3.4 %copy-done.4 = bf16[2048,2048]{1,0:T(8,128)(2,1)S(1)} copy-done((bf16[2048,2048]{1,0:T(8,128)(2,1)S(1)}, bf16[2048,2048]{1,0:T(8,128)(2,1)}, u32[]{:S(2)}) %copy-start.4) | copy-done | bytes 8388632
  92.7 0.0 copy-start.6
  92.7 0.9 copy-done.6
  93.6 6.8 %index_backward.1 = (bf16[4,32,2176]{2,1,0:T(8,128)(2,1)S(1)}, bf16[2048,128]{1,0:T(8,128)(2,1)}) custom-call(s32[3]{0:T(128)S(1)} %copy-done.1, bf16[4,32,2048]{2,1,0:T(8,128)(2,1)S(1)} %all-to-all-done.2.parts_ref, f32[32,2048]{1,0:T(8,128)S(1)} %copy-done.6, f32[32,1]{1,0:T(8,128)S(1)} %copy.21.kl_ref, bf16[2048,2048]{1,0:T(8,128)(2,1)S(1)} %copy-done.4, ...), custom_call_target="tpu_custom_call" | custom-call | flops 4294967296 | bytes 10485760 | tf_op jit(solution)/shard_map/index_backward/pallas_call | solution.py:246
  100.5 14.7 %all_to_all.27 = bf16[4,32,2176]{2,1,0:T(8,128)(2,1)S(1)} all-to-all(bf16[4,32,2176]{2,1,0:T(8,128)(2,1)S(1)} %get-tuple-element.11), channel_id=1, replica_groups=mesh['ctx_0'=2,'ctx_1'=4,'ctx_2'=4,'far'=2,'core'=2] {'far','core'}, dimensions={0} | all-to-all | bytes 1114112 | tf_op jit(solution)/shard_map/all_to_all | solution.py:320
  115.2 4.0 %all-to-all-start.4 = ((bf16[128,16,128]{2,1,0:T(8,128)(2,1)}), bf16[128,16,128]{2,1,0:T(8,128)(2,1)S(1)}, u32[]{:S(2)}, u32[]{:S(2)}) async-start(bf16[128,16,128]{2,1,0:T(8,128)(2,1)} %bitcast.13), calls=%async_computation.4 | async-start | bytes 1048576 | tf_op jit(solution)/shard_map/all_to_all | solution.py:318
  119.2 0.1 bitcast_convert_fusion
  119.3 1.1 slice.8
  120.4 0.7 copy.24
  121.0 11.7 %all-to-all-done.4 = bf16[128,16,128]{2,1,0:T(8,128)(2,1)S(1)} async-done(((bf16[128,16,128]{2,1,0:T(8,128)(2,1)}), bf16[128,16,128]{2,1,0:T(8,128)(2,1)S(1)}, u32[]{:S(2)}, u32[]{:S(2)}) %all-to-all-start.4) | async-done | bytes 524320 | tf_op jit(solution)/shard_map/all_to_all | solution.py:318
  132.7 0.7 convert_reduce_fusion
  (3 shorter events, 0.0 us)
Async XLA Ops:
  0.6 17.7 %copy-start = (bf16[64,576]{1,0:T(8,128)(2,1)S(1)}, bf16[64,576]{1,0:T(8,128)(2,1)}, u32[]{:S(2)}) copy-start(bf16[64,576]{1,0:T(8,128)(2,1)} %param.9) | copy-start | bytes 221188
  39.6 7.9 %copy-start.7 = (bf16[32,32,576]{2,1,0:T(8,128)(2,1)}, bf16[32,32,576]{2,1,0:T(8,128)(2,1)S(1)}, u32[]{:S(2)}) copy-start(bf16[32,32,576]{2,1,0:T(8,128)(2,1)S(1)} %all_to_all.26) | copy-start | bytes 3538948
  41.1 6.5 %collective-permute-start = (bf16[1024,576]{0,1:T(8,128)(2,1)}, bf16[1024,576]{0,1:T(8,128)(2,1)}, u32[]{:S(2)}, u32[]{:S(2)}) collective-permute-start(bf16[1024,576]{0,1:T(8,128)(2,1)} %copy.18), channel_id=1, source_target_pairs={{0,1},{1,0},{2,3},{3,2},{4,5},{5,4},{6,7},{7,6},{8,9},{9,8},{10,11... | collective-permute-start | bytes 3538952 | tf_op jit(solution)/shard_map/ppermute | solution.py:290
  46.7 33.1 %collective-permute-start.1 = (bf16[1024,128]{1,0:T(8,128)(2,1)S(1)}, bf16[1024,128]{1,0:T(8,128)(2,1)S(1)}, u32[]{:S(2)}, u32[]{:S(2)}) collective-permute-start(bf16[1024,128]{1,0:T(8,128)(2,1)S(1)} %bitcast.19), channel_id=1, source_target_pairs={{0,1},{1,0},{2,3},{3,2},{4,5},{5,4},{6,7},{7,6},{8,9},{9,8},{10,11... | collective-permute-start | bytes 786440 | tf_op jit(solution)/shard_map/ppermute | solution.py:290
  50.0 29.5 %copy-start.9 = (f32[128]{0:T(128)S(1)}, f32[128]{0:T(128)}, u32[]{:S(2)}) copy-start(f32[128]{0:T(128)} %param.13) | copy-start | bytes 1540
  50.0 29.6 %copy-start.8 = (f32[128,64]{0,1:T(8,128)S(1)}, f32[128,64]{0,1:T(8,128)}, u32[]{:S(2)}) copy-start(f32[128,64]{0,1:T(8,128)} %param.11) | copy-start | bytes 98308
  50.0 29.8 %copy-start.1 = (s32[3]{0:T(128)S(1)}, s32[3]{0:T(128)}, u32[]{:S(2)}) copy-start(s32[3]{0:T(128)} %pad_add_fusion.where) | copy-start | bytes 40
  50.0 29.8 %copy-start.2 = (bf16[128,8192]{1,0:T(8,128)(2,1)S(1)}, bf16[128,8192]{1,0:T(8,128)(2,1)}, u32[]{:S(2)}) copy-start(bf16[128,8192]{1,0:T(8,128)(2,1)} %q_ref.3) | copy-start | bytes 6291460
  74.2 15.1 %all-to-all-start.2 = ((bf16[4,32,2048]{2,1,0:T(8,128)(2,1)}), bf16[4,32,2048]{2,1,0:T(8,128)(2,1)S(1)}, u32[]{:S(2)}, u32[]{:S(2)}) async-start(bf16[4,32,2048]{2,1,0:T(8,128)(2,1)} %bitcast.26), calls=%async_computation.2 | async-start | bytes 1048576 | tf_op jit(solution)/shard_map/all_to_all | solution.py:314
  85.4 3.2 %copy-start.3 = (bf16[2048,2048]{1,0:T(8,128)(2,1)}, bf16[2048,2048]{1,0:T(8,128)(2,1)S(1)}, u32[]{:S(2)}) copy-start(bf16[2048,2048]{1,0:T(8,128)(2,1)S(1)} %get-tuple-element.10.mask_ref) | copy-start | bytes 25165828
  88.6 0.7 copy-start.5
  89.3 3.4 %copy-start.4 = (bf16[2048,2048]{1,0:T(8,128)(2,1)S(1)}, bf16[2048,2048]{1,0:T(8,128)(2,1)}, u32[]{:S(2)}) copy-start(bf16[2048,2048]{1,0:T(8,128)(2,1)} %copy-done.3) | copy-start | bytes 25165828
  92.7 0.9 copy-start.6
  115.2 17.5 %all-to-all-start.4 = ((bf16[128,16,128]{2,1,0:T(8,128)(2,1)}), bf16[128,16,128]{2,1,0:T(8,128)(2,1)S(1)}, u32[]{:S(2)}, u32[]{:S(2)}) async-start(bf16[128,16,128]{2,1,0:T(8,128)(2,1)} %bitcast.13), calls=%async_computation.4 | async-start | bytes 1048576 | tf_op jit(solution)/shard_map/all_to_all | solution.py:318

commit v2 on v1

v2 whole, which is shorter than its diff:
```python
import math

import jax
import jax.numpy as jnp
from jax import lax
from jax.experimental import pallas as pl
from jax.experimental.pallas import tpu as pltpu
from jax.sharding import Mesh
from jax.sharding import PartitionSpec as P

CTX = ("ctx_0", "ctx_1", "ctx_2")
HEAD = ("far", "core")
ALL = CTX + HEAD

LATENT = 576
MAIN_SCALE = 192.0 ** (-0.5)
LOG2E = math.log2(math.e)
bf16, f32 = jnp.bfloat16, jnp.float32

SIDES = 2


def key_of(place):
    half, side, ctx = place >> 10, (place >> 9) & 1, (place >> 4) & 31
    return ctx * 64 + half * 32 + side * 16 + (place & 15)


def lay_index_keys(keys, pieces, core):
    count = pieces[0].shape[0]
    for n, piece in enumerate(pieces):
        spot = ((core ^ (n // SIDES)) * SIDES + n % SIDES) * count
        keys[pl.ds(pl.multiple_of(spot, count), count), :] = piece[...]


def index_key_specs(own):
    first = own.shape[1] // IDX_DIM - SIDES
    return [
        pl.BlockSpec((own.shape[0], IDX_DIM), lambda g, where, at=first + side: (0, at))
        for _ in range(2)
        for side in range(SIDES)
    ]


def head_kernel(where, q_hbm, own_hbm, other_hbm, *refs):
    outs, (keys, queries, pair, scores, probs, acc, turned, sems) = refs[:4], refs[4:]
    pairs, rows, both_width = queries.shape
    width = both_width // 2
    count = own_hbm.shape[0]
    n_keys = 2 * SIDES * count
    wide = keys.shape[1] - rows
    body = wide - rows

    def key_copies(k, source):
        for side in range(SIDES):
            spot = ((where[0] ^ k) * SIDES + side) * count
            at = pl.ds(pl.multiple_of(spot, count), count)
            sem = (k * SIDES + side) * 2
            yield pltpu.make_async_copy(
                source.at[:, pl.ds(side * body, body)], keys.at[at, pl.ds(0, body)], sems.at[sem]
            )
            yield pltpu.make_async_copy(
                source.at[:, pl.ds(SIDES * body, rows)],
                keys.at[at, pl.ds(body, rows)],
                sems.at[sem + 1],
            )

    def query_copy(p):
        at = pl.multiple_of(p * both_width, 128)
        return pltpu.make_async_copy(
            q_hbm.at[:, pl.ds(at, both_width)], queries.at[p], sems.at[8 + p]
        )

    for k, source in enumerate((own_hbm, other_hbm)):
        for copy in key_copies(k, source):
            copy.start()
    query_copy(0).start()
    for p in range(1, pairs):
        query_copy(p).start()
    place = lax.broadcasted_iota(jnp.int32, (n_keys, rows), 0)
    query = lax.broadcasted_iota(jnp.int32, (n_keys, rows), 1)
    keys[:, wide:] = jnp.where(key_of(place) > query + where[1], -1e30, 0.0).astype(bf16)
    row = lax.broadcasted_iota(jnp.int32, (2 * rows, rows), 0)
    lane = lax.broadcasted_iota(jnp.int32, (2 * rows, rows), 1)
    pair[:, wide:] = jnp.where((row & (rows - 1)) == lane, 1.0, 0.0).astype(bf16)
    acc[...] = jnp.zeros(acc.shape, f32)
    scale = MAIN_SCALE * LOG2E
    vec = (8, 2 * rows)
    tall = (n_keys // 8, 8, 2 * rows)
    for k, source in enumerate((own_hbm, other_hbm)):
        for copy in key_copies(k, source):
            copy.wait()
    lane = lax.broadcasted_iota(jnp.int32, (count, rows), 1)
    for n in range(2 * SIDES):
        at = slice(n * count, (n + 1) * count)
        rest = keys[at, body:wide].astype(f32)
        keys[at, body:wide] = jnp.where(lane // (wide - width) == n % SIDES, rest, 0.0).astype(bf16)

    def add_pair(recip):
        old = (probs[...].astype(f32).reshape(tall) * recip[None]).reshape(n_keys, 2 * rows)
        acc[...] += old[:, :rows] + old[:, rows:]

    def step(p, carry):
        shift, recip = carry
        last = jnp.minimum(p, pairs - 1)

        @pl.when(p < pairs)
        def _():
            query_copy(p).wait()

        both = queries[last]
        for h in range(2):
            at = slice(h * rows, (h + 1) * rows)
            pair[at, 0:width] = both[:, h * width : (h + 1) * width]
            pair[at, width:wide] = both[:, h * width + body : (h + 1) * width]
        add_pair(recip)
        e = jnp.exp2(scores[...].reshape(tall) * scale - shift[None])
        total = jnp.sum(e, axis=0)
        probs[...] = e.reshape(n_keys, 2 * rows).astype(bf16)
        new = lax.dot_general(
            keys[...], pair[...], (((1,), (1,)), ((), ())), preferred_element_type=f32
        )
        scores[...] = new
        top = jnp.max(new.reshape(tall), axis=0)
        top = jnp.broadcast_to(jnp.max(top, axis=0, keepdims=True), vec)
        total = jnp.broadcast_to(jnp.sum(total, axis=0, keepdims=True), vec)
        return top * scale, jnp.where(p > 0, 1.0 / total, 0.0)

    scores[...] = jnp.zeros(scores.shape, f32)
    probs[...] = jnp.zeros(probs.shape, bf16)
    zero = jnp.zeros(vec, f32)
    _, recip = lax.fori_loop(0, pairs + 1, step, (zero, zero))
    add_pair(recip)
    turned[...] = (acc[...] * (1.0 / 128.0)).T.astype(bf16)
    few = rows // 4
    for k in range(4):
        outs[k][...] = turned[pl.ds(pl.multiple_of((where[2] ^ k) * few, few), few), :]


def head_totals(where, q, own, other):
    rows, columns = q.shape
    n_keys = 2 * SIDES * own.shape[0]
    pairs = columns // (2 * LATENT)
    vmem = pl.BlockSpec(memory_space=pltpu.VMEM)
    anywhere = pl.BlockSpec(memory_space=pl.ANY)
    return pl.pallas_call(
        head_kernel,
        out_shape=[jax.ShapeDtypeStruct((rows // 4, n_keys), bf16)] * 4,
        in_specs=[
            pl.BlockSpec(memory_space=pltpu.SMEM),
            pl.BlockSpec(memory_space=pltpu.HBM),
            anywhere,
            anywhere,
        ],
        out_specs=[vmem] * 4,
        scratch_shapes=[
            pltpu.VMEM((n_keys, 768), bf16),
            pltpu.VMEM((pairs, rows, 2 * LATENT), bf16),
            pltpu.VMEM((2 * rows, 768), bf16),
            pltpu.VMEM((n_keys, 2 * rows), f32),
            pltpu.VMEM((n_keys, 2 * rows), bf16),
            pltpu.VMEM((n_keys, rows), f32),
            pltpu.VMEM((rows, n_keys), bf16),
            pltpu.SemaphoreType.DMA((8 + pairs,)),
        ],
        compiler_params=pltpu.CompilerParams(vmem_limit_bytes=56 * 2**20),
        cost_estimate=pl.CostEstimate(
            flops=2 * 32 * rows * n_keys * 768, bytes_accessed=8 * 2**20, transcendentals=2**23
        ),
        name="head_totals",
    )(where, q, own, other)


IDX_GROUP = 32
IDX_DIM = 128
OWN_HEADS = 16
BIT = [1 << j for j in range(31)] + [-(2**31)]


def forward_kernel(where, q_ref, w_ref, *refs):
    pieces, (kl_ref, bits_ref, chance_ref, keys, block, logits) = refs[:4], refs[4:]
    g = pl.program_id(0)
    rows, dim = q_ref.shape[0], keys.shape[1]

    @pl.when(g == 0)
    def _():
        lay_index_keys(keys, pieces, where[0])
        logits[...] = jnp.zeros(logits.shape, f32)

    for j in range(IDX_GROUP):
        block[j * rows : (j + 1) * rows, :] = q_ref[:, j * dim : (j + 1) * dim]
    inner = lax.dot_general(
        block[...], keys[...], (((1,), (1,)), ((), ())), preferred_element_type=f32
    )
    weights = w_ref[0] * (dim ** (-0.5))
    total = logits[...]
    bits = jnp.zeros(total.shape, jnp.int32)
    for j in range(IDX_GROUP):
        part = inner[j * rows : (j + 1) * rows]
        total += jnp.maximum(part, 0.0) * weights[:, j : j + 1]
        bits = bits | jnp.where(part > 0.0, BIT[j], 0)
    logits[...] = total
    bits_ref[...] = bits

    @pl.when(g == pl.num_programs(0) - 1)
    def _():
        place = lax.broadcasted_iota(jnp.int32, logits.shape, 1)
        query = lax.broadcasted_iota(jnp.int32, logits.shape, 0) + where[2] * rows
        seen = key_of(place) <= query + where[1]
        values = jnp.where(seen, total, -1e30)
        e = jnp.where(seen, jnp.exp(values - jnp.max(values, axis=1, keepdims=True)), 0.0)
        chance_ref[...] = e * (kl_ref[...] / jnp.sum(e, axis=1, keepdims=True))


def index_forward(where, q, w, own, other, kl):
    rows, dim = kl.shape[0], IDX_DIM
    n_keys = 2 * SIDES * own.shape[0]
    heads = q.shape[1] // dim
    wide = IDX_GROUP * dim
    return pl.pallas_call(
        forward_kernel,
        grid_spec=pltpu.PrefetchScalarGridSpec(
            num_scalar_prefetch=1,
            grid=(heads // IDX_GROUP,),
            in_specs=[
                pl.BlockSpec((rows, wide), lambda g, where: (0, g)),
                pl.BlockSpec((1, rows, IDX_GROUP), lambda g, where: (g, 0, 0)),
                *index_key_specs(own),
                pl.BlockSpec((rows, 1), lambda g, where: (0, 0)),
            ],
            out_specs=[
                pl.BlockSpec((rows, n_keys), lambda g, where: (g, 0)),
                pl.BlockSpec((rows, n_keys), lambda g, where: (0, 0)),
            ],
            scratch_shapes=[
                pltpu.VMEM((n_keys, dim), bf16),
                pltpu.VMEM((IDX_GROUP * rows, dim), bf16),
                pltpu.VMEM((rows, n_keys), f32),
            ],
        ),
        out_shape=[
            jax.ShapeDtypeStruct((heads // IDX_GROUP * rows, n_keys), jnp.int32),
            jax.ShapeDtypeStruct((rows, n_keys), f32),
        ],
        compiler_params=pltpu.CompilerParams(vmem_limit_bytes=24 * 2**20),
        cost_estimate=pl.CostEstimate(
            flops=2 * heads * rows * n_keys * 256, bytes_accessed=10 * 2**20, transcendentals=2**16
        ),
        name="index_forward",
    )(where, q, w, own, own, other, other, kl)


def lay_masked(bits_ref, upstream, masked):
    rows = bits_ref.shape[0]
    bits, up = bits_ref[...], upstream[...]
    for j in range(IDX_GROUP):
        masked[j * rows : (j + 1) * rows, :] = jnp.where(bits & BIT[j] != 0, up, 0.0).astype(bf16)


def query_kernel(where, upstream_ref, bits_ref, q_ref, w_ref, *refs):
    pieces, outs, (keys, masked, grad_ref) = refs[:4], refs[4:8], refs[8:]
    g = pl.program_id(0)
    rows, dim = q_ref.shape[0], keys.shape[1]
    wide = grad_ref.shape[2] - 128

    @pl.when(g == 0)
    def _():
        lay_index_keys(keys, pieces, where[0])

    lay_masked(bits_ref, upstream_ref, masked)
    plain = lax.dot_general(
        masked[...], keys[...], (((1,), (0,)), ((), ())), preferred_element_type=f32
    ) * (dim ** (-0.5))
    lane = lax.broadcasted_iota(jnp.int32, (rows, 128), 1)
    for first in range(0, IDX_GROUP, OWN_HEADS):
        owner = g * (IDX_GROUP // OWN_HEADS) + first // OWN_HEADS
        sums = jnp.zeros((rows, 128), f32)
        for n in range(OWN_HEADS):
            j = first + n
            q = q_ref[:, j * dim : (j + 1) * dim].astype(f32)
            part = plain[j * rows : (j + 1) * rows]
            gain = w_ref[0, :, j : j + 1]
            grad_ref[owner, :, n * dim : (n + 1) * dim] = (part * gain).astype(bf16)
            sums = jnp.where(lane == n, jnp.sum(q * part, axis=1, keepdims=True), sums)
        grad_ref[owner, :, wide:] = sums.astype(bf16)

    @pl.when(g == pl.num_programs(0) - 1)
    def _():
        for k in range(4):
            outs[k][...] = grad_ref[where[2] ^ k]


def key_kernel(where, *refs):
    parts, refs = refs[:4], refs[4:]
    chance_ref, kl_ref, bits_ref, q_ref, w_ref, gk_ref, upstream_ref, masked, block, acc = refs
    g = pl.program_id(0)
    rows, dim = q_ref.shape[0], block.shape[1]

    @pl.when(g == 0)
    def _():
        target = parts[0][...].astype(f32)
        for k in range(1, 4):
            target += parts[k][...].astype(f32)
        upstream_ref[...] = chance_ref[...] - kl_ref[...] * target
        acc[...] = jnp.zeros(acc.shape, f32)

    lay_masked(bits_ref, upstream_ref, masked)
    for j in range(IDX_GROUP):
        q = q_ref[:, j * dim : (j + 1) * dim].astype(f32)
        block[j * rows : (j + 1) * rows, :] = (q * w_ref[0, :, j : j + 1]).astype(bf16)
    acc[...] += lax.dot_general(
        block[...], masked[...], (((0,), (0,)), ((), ())), preferred_element_type=f32
    )

    @pl.when(g == pl.num_programs(0) - 1)
    def _():
        for t in range(acc.shape[1] // 128):
            piece = (acc[:, t * 128 : (t + 1) * 128] * (dim ** (-0.5))).T.astype(bf16)
            for b in range(0, 128, 16):
                key = key_of(t * 128 + b)
                gk_ref[key : key + 16, :] = piece[b : b + 16]


def whole(*shape):
    return pl.BlockSpec(shape, lambda g, where: (0,) * len(shape))


def index_query_grads(where, upstream, bits, q, w, own, other):
    rows, n_keys = upstream.shape
    dim = IDX_DIM
    heads = q.shape[1] // dim
    out = jax.ShapeDtypeStruct((rows, heads // 4 * dim + 128), bf16)
    return pl.pallas_call(
        query_kernel,
        grid_spec=pltpu.PrefetchScalarGridSpec(
            num_scalar_prefetch=1,
            grid=(heads // IDX_GROUP,),
            in_specs=[
                whole(rows, n_keys),
                pl.BlockSpec((rows, n_keys), lambda g, where: (g, 0)),
                pl.BlockSpec((rows, IDX_GROUP * dim), lambda g, where: (0, g)),
                pl.BlockSpec((1, rows, IDX_GROUP), lambda g, where: (g, 0, 0)),
                *index_key_specs(own),
            ],
            out_specs=[whole(*out.shape)] * 4,
            scratch_shapes=[
                pltpu.VMEM((n_keys, dim), bf16),
                pltpu.VMEM((IDX_GROUP * rows, n_keys), bf16),
                pltpu.VMEM((4, *out.shape), bf16),
            ],
        ),
        out_shape=[out] * 4,
        compiler_params=pltpu.CompilerParams(vmem_limit_bytes=24 * 2**20),
        cost_estimate=pl.CostEstimate(
            flops=4 * heads * rows * n_keys * 128, bytes_accessed=6 * 2**20, transcendentals=0
        ),
        name="index_query_grads",
    )(where, upstream, bits, q, w, own, own, other, other)


def index_key_grads(where, parts, chance, kl, bits, q, w):
    rows, n_keys = chance.shape
    dim = IDX_DIM
    heads = q.shape[1] // dim
    return pl.pallas_call(
        key_kernel,
        grid_spec=pltpu.PrefetchScalarGridSpec(
            num_scalar_prefetch=1,
            grid=(heads // IDX_GROUP,),
            in_specs=[
                *[whole(rows, n_keys)] * 5,
                whole(rows, 1),
                pl.BlockSpec((rows, n_keys), lambda g, where: (g, 0)),
                pl.BlockSpec((rows, IDX_GROUP * dim), lambda g, where: (0, g)),
                pl.BlockSpec((1, rows, IDX_GROUP), lambda g, where: (g, 0, 0)),
            ],
            out_specs=[whole(n_keys, dim), whole(rows, n_keys)],
            scratch_shapes=[
                pltpu.VMEM((IDX_GROUP * rows, n_keys), bf16),
                pltpu.VMEM((IDX_GROUP * rows, dim), bf16),
                pltpu.VMEM((dim, n_keys), f32),
            ],
        ),
        out_shape=[
            jax.ShapeDtypeStruct((n_keys, dim), bf16),
            jax.ShapeDtypeStruct((rows, n_keys), f32),
        ],
        compiler_params=pltpu.CompilerParams(vmem_limit_bytes=24 * 2**20),
        cost_estimate=pl.CostEstimate(
            flops=4 * heads * rows * n_keys * 128, bytes_accessed=6 * 2**20, transcendentals=0
        ),
        name="index_key_grads",
    )(where, *parts, chance, kl, bits, q, w)


def to_all(piece, axes):
    copies = jnp.broadcast_to(piece, (lax.axis_size(axes), *piece.shape))
    return lax.all_to_all(copies, axes, split_axis=0, concat_axis=0, tiled=True)


def finish_kernel(where, *refs):
    grads, (key_ref, query_out, weight_out, key_out, wide_weight) = refs[:4], refs[4:]
    few, wide = grads[0].shape[0], query_out.shape[1]
    for k in range(4):
        at = pl.ds(pl.multiple_of((where[2] ^ k) * few, few), few)
        query_out[at, :] = grads[k][:, :wide].astype(f32)
        wide_weight[at, :] = grads[k][:, wide:].astype(f32)
    weight_out[...] = wide_weight[...].T[: weight_out.shape[0]]
    key_out[...] = jnp.sum(key_ref[...].astype(f32), axis=0)


def finish(where, grads, keys):
    rows = 4 * grads[0].shape[0]
    vmem = pl.BlockSpec(memory_space=pltpu.VMEM)
    return pl.pallas_call(
        finish_kernel,
        out_shape=[
            jax.ShapeDtypeStruct((rows, OWN_HEADS * IDX_DIM), f32),
            jax.ShapeDtypeStruct((OWN_HEADS, rows), f32),
            jax.ShapeDtypeStruct(keys.shape[1:], f32),
        ],
        in_specs=[pl.BlockSpec(memory_space=pltpu.SMEM)] + [vmem] * 5,
        out_specs=[vmem] * 3,
        scratch_shapes=[pltpu.VMEM((rows, 128), f32)],
        compiler_params=pltpu.CompilerParams(vmem_limit_bytes=16 * 2**20),
        cost_estimate=pl.CostEstimate(flops=2**20, bytes_accessed=2**21, transcendentals=0),
        name="finish",
    )(where, *grads, keys)


def swap_heads(pieces):
    count = len(pieces)
    return [pieces[0]] + [
        lax.ppermute(pieces[k], HEAD, [(h, h ^ k) for h in range(count)]) for k in range(1, count)
    ]


def shards(
    main_query, latents, idx_query, idx_weight, idx_keys, kl_cotangent, query_start, key_start
):
    rows = main_query.shape[0]
    core = lax.axis_index("core")
    head = lax.axis_index(HEAD)
    few = rows // lax.axis_size(HEAD)
    offset = query_start[0] + lax.axis_index(CTX) * rows - key_start[0]
    where = jnp.stack([core, offset, head]).astype(jnp.int32)

    half, side = latents.shape[0] // 2, latents.shape[0] // 4
    body = latents.shape[1] // 128 * 128
    lat = lax.dynamic_slice_in_dim(latents, core * half, half, 0)
    idx = lax.dynamic_slice_in_dim(idx_keys, core * half, half, 0)
    parts = [lat[:, :body], lat[:, body:], idx]
    slab = jnp.concatenate([p[at : at + side] for p in parts for at in (0, side)], axis=1)
    own = to_all(slab, CTX).reshape(-1, slab.shape[1])
    other = lax.ppermute(own, "core", [(0, 1), (1, 0)])

    kl = lax.dynamic_slice_in_dim(kl_cotangent, head * few, few, 0)[:, None]
    w = lax.dynamic_slice_in_dim(idx_weight, head * few, few, 0)
    w = w.reshape(few, -1, IDX_GROUP).transpose(1, 0, 2)

    few_queries = lax.dynamic_slice_in_dim(idx_query, head * few, few, 0)

    parts = swap_heads(head_totals(where, main_query, own, other))
    bits, chance = index_forward(where, few_queries, w, own, other, kl)
    gk, upstream = index_key_grads(where, parts, chance, kl, bits, few_queries, w)
    pieces = lax.all_to_all(gk.reshape(lax.axis_size(ALL), -1, gk.shape[1]), ALL, 0, 0, tiled=True)
    grads = index_query_grads(where, upstream, bits, few_queries, w, own, other)
    grad_query, grad_weight, grad_keys = finish(where, swap_heads(grads), pieces)
    return grad_query, grad_weight.T, grad_keys


def solution(mesh):
    torus = Mesh(mesh.devices.reshape(2, 4, 4, 2, 2), ALL)
    placed = (
        P(CTX, HEAD),
        P(CTX, None),
        P(CTX, None),
        P(CTX, None),
        P(CTX, None),
        P(CTX),
        P(),
        P(),
    )
    return jax.shard_map(
        shards,
        mesh=torus,
        in_specs=placed,
        out_specs=(P(CTX, HEAD), P(CTX, HEAD), P(ALL, None)),
        check_vma=False,
    )
```

time: 134 us -> 111 us (0.83)
  blocking collectives: 52.8 us -> 28.7 us
  waiting for transfers between devices: 12.5 us -> 6.97 us
  Pallas kernels: 36.6 us -> 41.1 us
  starting transfers between devices: 12.8 us -> 17.2 us
  local copies, waits for them, and re-layouts: 15.1 us -> 13.2 us
    all_to_all x1 -> x0, blocking collectives: 14.7 us -> none  [shards(): lax.all_to_all(grad, HEAD, 0, 0, tiled=True).reshape(rows, -1).astype(f32)]
    all_to_all x1, waiting for transfers between devices: 11.7 us -> 0.01 us  [shards(): lax.all_to_all(gk.reshape(lax.axis_size(ALL), -1, gk.shape[1]), ALL, 0, 0...]
    all_to_all x2 -> x1, blocking collectives: 38.1 us -> 28.7 us  [to_all(): return lax.all_to_all(copies, axes, split_axis=0, concat_axis=0, tiled=True)]
    ppermute x2 -> x7, starting transfers between devices: 3.64 us -> 10.8 us  [the longest x6 8.17 us: swap_heads(): lax.ppermute(pieces[k], HEAD, [(h, h ^ k) for h in range(count)])]
    ppermute x2 -> x7, waiting for transfers between devices: 0.86 us -> 6.96 us  [the longest x6 6.96 us: swap_heads(): lax.ppermute(pieces[k], HEAD, [(h, h ^ k) for h in range(count)])]
    all_to_all x1 -> x0, starting transfers between devices: 5.23 us -> none  [shards(): lax.all_to_all(target.reshape(heads, few, -1), HEAD, 0, 0, tiled=True)]
    pallas_call x2 -> x4, Pallas kernels: 31 us -> 35.2 us  [the longest x1 23.8 us: head_totals(): pl.pallas_call(head_kernel, out_shape=[jax.ShapeDtypeStruct((rows // 4, n...]
    all_to_all x1, starting transfers between devices: 3.97 us -> 6.47 us  [shards(): lax.all_to_all(gk.reshape(lax.axis_size(ALL), -1, gk.shape[1]), ALL, 0, 0...]
  transfers between devices with their start and end apart: 4 -> 8, of which waited for: 2 -> 3; matrix products, arithmetic and copies ran while one was open for 4% -> 4% of each run, Pallas kernels for 22% -> 9%
where the time goes in v2:
time: 111 us; the launch traced here: 110 us
  Pallas kernels  41.1 us (37%)
  blocking collectives  28.7 us (26%)
  starting transfers between devices  17.2 us (15%)
  local copies, waits for them, and re-layouts  13.2 us (12%)
  waiting for transfers between devices  6.97 us (6%)
  between operations  2.11 us (2%)
    all_to_all x1, blocking collectives, to_all(): return lax.all_to_all(copies, axes, split_axis=0, concat_axis=0, tiled=True)  28.7 us
    pallas_call x1, Pallas kernels, head_totals(): pl.pallas_call(head_kernel, out_shape=[jax.ShapeDtypeStruct((rows // 4, n...  23.8 us
    ppermute x6, starting transfers between devices, swap_heads(): lax.ppermute(pieces[k], HEAD, [(h, h ^ k) for h in range(count)])  8.17 us
    ppermute x6, waiting for transfers between devices, swap_heads(): lax.ppermute(pieces[k], HEAD, [(h, h ^ k) for h in range(count)])  6.96 us
    unnamed x32, local copies, waits for them, and re-layouts  6.49 us
    all_to_all x1, starting transfers between devices, shards(): lax.all_to_all(gk.reshape(lax.axis_size(ALL), -1, gk.shape[1]), ALL, 0, 0...  6.47 us
    pallas_call x1, Pallas kernels, index_forward(): pl.pallas_call(forward_kernel, grid_spec=pltpu.PrefetchScalarGridSpec(num...  5.9 us
    pallas_call x1, Pallas kernels, index_key_grads(): pl.pallas_call(key_kernel, grid_spec=pltpu.PrefetchScalarGridSpec(num_sca...  5.4 us
  transfers between devices with their start and end apart: 8, of which 3 were waited for; matrix products, arithmetic and copies ran while one was open for 4% of the time, Pallas kernels for 9%

profile of v2, /device:TPU:1, one launch (start us, length us, event | category | flops | bytes accessed | tf_op | source)
XLA Modules:
  0.0 110.0 jit_solution(6181210113734375946)
XLA Ops:
  0.6 0.0 copy-start
  0.7 0.9 constant_dynamic-slice_fusion
  1.5 0.7 fusion
  2.2 0.7 constant_dynamic-slice_fusion.4
  3.0 0.1 concatenate.3
  3.0 0.1 broadcast_in_dim.6
  3.2 28.7 %all_to_all.10 = bf16[32,16,1408]{2,1,0:T(8,128)(2,1)S(1)} all-to-all(bf16[32,16,1408]{2,1,0:T(8,128)(2,1)S(1)} %broadcast_in_dim.6), channel_id=1, replica_groups=mesh['ctx_0'=2,'ctx_1'=4,'ctx_2'=4,'far'=2,'core'=2] {'ctx_0','ctx_1','c..., dimensions={0} | all-to-all | bytes 2883584 | tf_op jit(solution)/shard_map/all_to_all | solution.py:397
  31.8 2.6 %collective-permute-start = (bf16[512,1408]{1,0:T(8,128)(2,1)S(1)}, bf16[512,1408]{1,0:T(8,128)(2,1)}, u32[]{:S(2)}, u32[]{:S(2)}) collective-permute-start(bf16[512,1408]{1,0:T(8,128)(2,1)S(1)} %bitcast.14), channel_id=1, source_target_pairs={{0,1},{1,0},{2,3},{3,2},{4,5},{5,4},{6,7},{7,6},{8,9},{9,8},{10,11... | collective-permute-start | bytes 4325384 | tf_op jit(solution)/shard_map/ppermute | solution.py:454
  35.7 0.0 copy-done.15
  35.7 0.6 dynamic-slice_bitcast_fusion
  36.3 0.7 copy.15.refs_4_.refs_5_
  37.0 1.4 %constant_dynamic-slice_fusion.2 = f32[32,64]{0,1:T(8,128)} fusion(f32[128,64]{0,1:T(8,128)} %param.11, s32[]{:T(128)S(6)} %select_n.10), kind=kLoop, calls=%fused_computation.2 | loop fusion | bytes 16388 | tf_op jit(solution)/shard_map/dynamic_slice | solution.py:457
  38.5 1.4 %copy.14 = f32[32,2,32]{2,0,1:T(8,128)} copy(f32[32,2,32]{0,2,1:T(8,128)} %bitcast.23) | data formatting | bytes 16384 | tf_op jit(solution)/shard_map/reshape | solution.py:458
  39.9 0.6 pad_add_fusion.where
  40.6 0.0 copy-done
  40.6 0.0 copy-start.4
  40.6 0.0 copy-start.6
  40.6 0.0 copy-start.8
  40.6 0.0 collective-permute-done.other_hbm.refs_2_.refs_3_
  40.7 0.0 copy-done.1
  40.7 23.8 %head_totals.1 = (bf16[32,2048]{1,0:T(8,128)(2,1)}, bf16[32,2048]{1,0:T(8,128)(2,1)}, bf16[32,2048]{1,0:T(8,128)(2,1)}, bf16[32,2048]{1,0:T(8,128)(2,1)}) custom-call(s32[3]{0:T(128)} %pad_add_fusion.where, bf16[128,18432]{1,0:T(8,128)(2,1)} %q_hbm.1, bf16[512,1408]{1,0:T(8,128)(2,1)} %bitcast.15, ...), custom_call_target="tpu_custom_call" | custom-call | flops 12884901888 | bytes 8388608 | tf_op jit(solution)/shard_map/head_totals/pallas_call | solution.py:145
  64.5 0.1 collective-permute-start.1
  64.6 3.4 %collective-permute-start.2 = (bf16[32,2048]{1,0:T(8,128)(2,1)}, bf16[32,2048]{1,0:T(8,128)(2,1)S(1)}, u32[]{:S(2)}, u32[]{:S(2)}) collective-permute-start(bf16[32,2048]{1,0:T(8,128)(2,1)} %get-tuple-element.20), channel_id=1, source_target_pairs={{0,2},{1,3},{2,0},{3,1},{4,6},{5,7},{6,4},{7,5},{8,10},{9,11},{10,... | collective-permute-start | bytes 393224 | tf_op jit(solution)/shard_map/ppermute | solution.py:433
  68.0 0.3 collective-permute-start.3
  68.3 0.0 copy-done.6
  68.3 1.4 %copy-done.2 = bf16[32,16,1408]{2,1,0:T(8,128)(2,1)S(1)} copy-done((bf16[32,16,1408]{2,1,0:T(8,128)(2,1)S(1)}, bf16[32,16,1408]{2,1,0:T(8,128)(2,1)}, u32[]{:S(2)}) %copy-start.2) | copy-done | bytes 1441816
  69.7 5.9 %index_forward.1 = (s32[64,2048]{1,0:T(8,128)S(1)}, f32[32,2048]{1,0:T(8,128)S(1)}) custom-call(s32[3]{0:T(128)S(1)} %copy-done.8, bf16[32,8192]{1,0:T(8,128)(2,1)S(1)} %constant_dynamic-slice_fusion.3.q_ref.refs_7_, f32[2,32,32]{2,1,0:T(8,128)S(1)} %bitcast.20, bf16[512,1408]{1,0:T(8,128)(2,1)S(1)} %bitcast.16, bf16[512,1408]{1,0:T(8,128)(2,1)S(1)} %bitcast.17, ...), custom_call_target="tpu_custom_call" | custom-call | flops 2147483648 | bytes 10485760 | tf_op jit(solution)/shard_map/index_forward/pallas_call | solution.py:219
  75.6 0.0 collective-permute-done.1.refs_1_
  75.6 0.0 collective-permute-done.2.refs_2_
  75.6 0.1 collective-permute-done.3.refs_3_
  75.8 0.0 copy-done.14
  75.8 5.4 %index_key_grads.1 = (bf16[2048,128]{1,0:T(8,128)(2,1)}, f32[32,2048]{1,0:T(8,128)S(1)}) custom-call(s32[3]{0:T(128)S(1)} %copy-done.8, bf16[32,2048]{1,0:T(8,128)(2,1)S(1)} %copy-done.14, bf16[32,2048]{1,0:T(8,128)(2,1)S(1)} %collective-permute-done.1.refs_1_, bf16[32,2048]{1,0:T(8,128)(2,1)S(1)} %collective-permute-done.2.refs_2_, ...), custom_call_target="tpu_custom_call" | custom-call | flops 2147483648 | bytes 6291456 | tf_op jit(solution)/shard_map/index_key_grads/pallas_call | solution.py:364
  81.2 0.0 copy-done.10
  81.2 0.7 copy-done.12
  81.9 6.5 %all-to-all-start.1 = ((bf16[128,16,128]{2,1,0:T(8,128)(2,1)}), bf16[128,16,128]{2,1,0:T(8,128)(2,1)S(1)}, u32[]{:S(2)}, u32[]{:S(2)}) async-start(bf16[128,16,128]{2,1,0:T(8,128)(2,1)} %bitcast.9), calls=%async_computation.1 | async-start | bytes 1048576 | tf_op jit(solution)/shard_map/all_to_all | solution.py:465
  88.4 1.4 %copy-done.3 = bf16[32,16,1408]{2,1,0:T(8,128)(2,1)S(1)} copy-done((bf16[32,16,1408]{2,1,0:T(8,128)(2,1)S(1)}, bf16[32,16,1408]{2,1,0:T(8,128)(2,1)}, u32[]{:S(2)}) %copy-start.3) | copy-done | bytes 1441816
  89.7 1.0 copy-done.5
  90.8 1.0 copy-done.11
  91.8 0.9 copy-done.13
  92.8 4.4 %index_query_grads.1 = (bf16[32,2176]{1,0:T(8,128)(2,1)S(1)}, bf16[32,2176]{1,0:T(8,128)(2,1)S(1)}, bf16[32,2176]{1,0:T(8,128)(2,1)S(1)}, bf16[32,2176]{1,0:T(8,128)(2,1)S(1)}) custom-call(s32[3]{0:T(128)S(1)} %copy-done.9, f32[32,2048]{1,0:T(8,128)S(1)} %copy-done.13, s32[64,2048]{1,0:T(8,128)S(1)} %copy-done.11, bf16[32,8192]{1,0:T(8,128)(2,1)S(1)} %copy-done.5, ...), custom_call_target="tpu_custom_call" | custom-call | flops 2147483648 | bytes 6291456 | tf_op jit(solution)/shard_map/index_query_grads/pallas_call | solution.py:332
  97.2 1.1 %collective-permute-start.4 = (bf16[32,2176]{1,0:T(8,128)(2,1)S(1)}, bf16[32,2176]{1,0:T(8,128)(2,1)S(1)}, u32[]{:S(2)}, u32[]{:S(2)}) collective-permute-start(bf16[32,2176]{1,0:T(8,128)(2,1)S(1)} %get-tuple-element.26), channel_id=1, source_target_pairs={{0,1},{1,0},{2,3},{3,2},{4,5},{5,4},{6,7},{7,6},{8,9},{9,8},{10,11... | collective-permute-start | bytes 417800 | tf_op jit(solution)/shard_map/ppermute | solution.py:433
  98.4 2.6 %collective-permute-start.5 = (bf16[32,2176]{1,0:T(8,128)(2,1)S(1)}, bf16[32,2176]{1,0:T(8,128)(2,1)S(1)}, u32[]{:S(2)}, u32[]{:S(2)}) collective-permute-start(bf16[32,2176]{1,0:T(8,128)(2,1)S(1)} %get-tuple-element.27), channel_id=1, source_target_pairs={{0,2},{1,3},{2,0},{3,1},{4,6},{5,7},{6,4},{7,5},{8,10},{9,11},{10,... | collective-permute-start | bytes 417800 | tf_op jit(solution)/shard_map/ppermute | solution.py:433
  100.9 0.7 collective-permute-start.6
  101.6 0.0 collective-permute-done.4.refs_1_
  101.6 3.5 %collective-permute-done.5.refs_2_ = bf16[32,2176]{1,0:T(8,128)(2,1)S(1)} collective-permute-done((bf16[32,2176]{1,0:T(8,128)(2,1)S(1)}, bf16[32,2176]{1,0:T(8,128)(2,1)S(1)}, u32[]{:S(2)}, u32[]{:S(2)}) %collective-permute-start.5) | collective-permute-done | bytes 139296 | tf_op jit(solution)/shard_map/ppermute | solution.py:433
  105.1 3.3 %collective-permute-done.6.refs_3_ = bf16[32,2176]{1,0:T(8,128)(2,1)S(1)} collective-permute-done((bf16[32,2176]{1,0:T(8,128)(2,1)S(1)}, bf16[32,2176]{1,0:T(8,128)(2,1)S(1)}, u32[]{:S(2)}, u32[]{:S(2)}) %collective-permute-start.6) | collective-permute-done | bytes 139296 | tf_op jit(solution)/shard_map/ppermute | solution.py:433
  108.4 0.0 all-to-all-done.1.refs_4_
  108.4 1.6 %finish.1 = (f32[128,2048]{1,0:T(8,128)}, f32[16,128]{1,0:T(8,128)}, f32[16,128]{1,0:T(8,128)}) custom-call(s32[3]{0:T(128)S(1)} %copy-done.9, bf16[32,2176]{1,0:T(8,128)(2,1)S(1)} %get-tuple-element.25.refs_0_, bf16[32,2176]{1,0:T(8,128)(2,1)S(1)} %collective-permute-done.4.refs_1_, bf16[32,2176]{1,0:T(8,128)(2,1)S(1)} %collective-permute-done.5.refs_2_, ...), custom_call_target="tpu_custom_call" | custom-call | flops 1048576 | bytes 2097152 | tf_op jit(solution)/shard_map/finish/pallas_call | solution.py:414
  (17 shorter events, 0.1 us)
Async XLA Ops:
  0.6 39.9 %copy-start = (bf16[128,8192]{1,0:T(8,128)(2,1)S(1)}, bf16[128,8192]{1,0:T(8,128)(2,1)}, u32[]{:S(2)}) copy-start(bf16[128,8192]{1,0:T(8,128)(2,1)} %param.10) | copy-start | bytes 6291460
  3.0 32.7 %copy-start.15 = (f32[128]{0:T(128)S(1)}, f32[128]{0:T(128)}, u32[]{:S(2)}) copy-start(f32[128]{0:T(128)} %param.13) | copy-start | bytes 1540
  31.8 8.8 %copy-start.1 = (bf16[32,16,1408]{2,1,0:T(8,128)(2,1)}, bf16[32,16,1408]{2,1,0:T(8,128)(2,1)S(1)}, u32[]{:S(2)}) copy-start(bf16[32,16,1408]{2,1,0:T(8,128)(2,1)S(1)} %all_to_all.10) | copy-start | bytes 4325380
  31.8 8.8 %collective-permute-start = (bf16[512,1408]{1,0:T(8,128)(2,1)S(1)}, bf16[512,1408]{1,0:T(8,128)(2,1)}, u32[]{:S(2)}, u32[]{:S(2)}) collective-permute-start(bf16[512,1408]{1,0:T(8,128)(2,1)S(1)} %bitcast.14), channel_id=1, source_target_pairs={{0,1},{1,0},{2,3},{3,2},{4,5},{5,4},{6,7},{7,6},{8,9},{9,8},{10,11... | collective-permute-start | bytes 4325384 | tf_op jit(solution)/shard_map/ppermute | solution.py:454
  40.6 35.1 %copy-start.4 = (bf16[32,8192]{1,0:T(8,128)(2,1)}, bf16[32,8192]{1,0:T(8,128)(2,1)S(1)}, u32[]{:S(2)}) copy-start(bf16[32,8192]{1,0:T(8,128)(2,1)S(1)} %constant_dynamic-slice_fusion.3.q_ref.refs_7_) | copy-start | bytes 1572868
  40.6 27.7 %copy-start.6 = (f32[32,2,32]{2,0,1:T(8,128)S(1)}, f32[32,2,32]{2,0,1:T(8,128)}, u32[]{:S(2)}) copy-start(f32[32,2,32]{2,0,1:T(8,128)} %copy.14) | copy-start | bytes 24580
  40.6 27.7 %copy-start.8 = (s32[3]{0:T(128)S(1)}, s32[3]{0:T(128)}, u32[]{:S(2)}) copy-start(s32[3]{0:T(128)} %pad_add_fusion.where) | copy-start | bytes 40
  64.5 11.1 %collective-permute-start.1 = (bf16[32,2048]{1,0:T(8,128)(2,1)}, bf16[32,2048]{1,0:T(8,128)(2,1)S(1)}, u32[]{:S(2)}, u32[]{:S(2)}) collective-permute-start(bf16[32,2048]{1,0:T(8,128)(2,1)} %get-tuple-element.19), channel_id=1, source_target_pairs={{0,1},{1,0},{2,3},{3,2},{4,5},{5,4},{6,7},{7,6},{8,9},{9,8},{10,11... | collective-permute-start | bytes 393224 | tf_op jit(solution)/shard_map/ppermute | solution.py:433
  64.6 11.0 %collective-permute-start.2 = (bf16[32,2048]{1,0:T(8,128)(2,1)}, bf16[32,2048]{1,0:T(8,128)(2,1)S(1)}, u32[]{:S(2)}, u32[]{:S(2)}) collective-permute-start(bf16[32,2048]{1,0:T(8,128)(2,1)} %get-tuple-element.20), channel_id=1, source_target_pairs={{0,2},{1,3},{2,0},{3,1},{4,6},{5,7},{6,4},{7,5},{8,10},{9,11},{10,... | collective-permute-start | bytes 393224 | tf_op jit(solution)/shard_map/ppermute | solution.py:433
  68.0 7.8 %collective-permute-start.3 = (bf16[32,2048]{1,0:T(8,128)(2,1)}, bf16[32,2048]{1,0:T(8,128)(2,1)S(1)}, u32[]{:S(2)}, u32[]{:S(2)}) collective-permute-start(bf16[32,2048]{1,0:T(8,128)(2,1)} %get-tuple-element.21), channel_id=1, source_target_pairs={{0,3},{1,2},{2,1},{3,0},{4,7},{5,6},{6,5},{7,4},{8,11},{9,10},{10,... | collective-permute-start | bytes 393224 | tf_op jit(solution)/shard_map/ppermute | solution.py:433
  68.3 1.4 %copy-start.2 = (bf16[32,16,1408]{2,1,0:T(8,128)(2,1)S(1)}, bf16[32,16,1408]{2,1,0:T(8,128)(2,1)}, u32[]{:S(2)}) copy-start(bf16[32,16,1408]{2,1,0:T(8,128)(2,1)} %copy-done.1) | copy-start | bytes 4325380
  69.7 6.1 %copy-start.14 = (bf16[32,2048]{1,0:T(8,128)(2,1)S(1)}, bf16[32,2048]{1,0:T(8,128)(2,1)}, u32[]{:S(2)}) copy-start(bf16[32,2048]{1,0:T(8,128)(2,1)} %get-tuple-element.18.refs_0_) | copy-start | bytes 393220
  75.6 5.6 %copy-start.10 = (s32[64,2048]{1,0:T(8,128)}, s32[64,2048]{1,0:T(8,128)S(1)}, u32[]{:S(2)}) copy-start(s32[64,2048]{1,0:T(8,128)S(1)} %get-tuple-element.23.refs_6_.bits_ref) | copy-start | bytes 1572868
  75.8 12.6 %copy-start.7 = (f32[32,2,32]{2,0,1:T(8,128)S(1)}, f32[32,2,32]{2,0,1:T(8,128)}, u32[]{:S(2)}) copy-start(f32[32,2,32]{2,0,1:T(8,128)} %copy.14) | copy-start | bytes 24580
  75.8 12.6 %copy-start.9 = (s32[3]{0:T(128)S(1)}, s32[3]{0:T(128)}, u32[]{:S(2)}) copy-start(s32[3]{0:T(128)} %pad_add_fusion.where) | copy-start | bytes 40
  81.2 0.7 copy-start.12
  81.9 26.5 %all-to-all-start.1 = ((bf16[128,16,128]{2,1,0:T(8,128)(2,1)}), bf16[128,16,128]{2,1,0:T(8,128)(2,1)S(1)}, u32[]{:S(2)}, u32[]{:S(2)}) async-start(bf16[128,16,128]{2,1,0:T(8,128)(2,1)} %bitcast.9), calls=%async_computation.1 | async-start | bytes 1048576 | tf_op jit(solution)/shard_map/all_to_all | solution.py:465
  88.4 1.4 %copy-start.3 = (bf16[32,16,1408]{2,1,0:T(8,128)(2,1)S(1)}, bf16[32,16,1408]{2,1,0:T(8,128)(2,1)}, u32[]{:S(2)}) copy-start(bf16[32,16,1408]{2,1,0:T(8,128)(2,1)} %copy-done.1) | copy-start | bytes 4325380
  89.7 1.0 copy-start.5
  90.8 1.0 copy-start.11
  91.8 0.9 copy-start.13
  97.2 4.4 %collective-permute-start.4 = (bf16[32,2176]{1,0:T(8,128)(2,1)S(1)}, bf16[32,2176]{1,0:T(8,128)(2,1)S(1)}, u32[]{:S(2)}, u32[]{:S(2)}) collective-permute-start(bf16[32,2176]{1,0:T(8,128)(2,1)S(1)} %get-tuple-element.26), channel_id=1, source_target_pairs={{0,1},{1,0},{2,3},{3,2},{4,5},{5,4},{6,7},{7,6},{8,9},{9,8},{10,11... | collective-permute-start | bytes 417800 | tf_op jit(solution)/shard_map/ppermute | solution.py:433
  98.4 6.7 %collective-permute-start.5 = (bf16[32,2176]{1,0:T(8,128)(2,1)S(1)}, bf16[32,2176]{1,0:T(8,128)(2,1)S(1)}, u32[]{:S(2)}, u32[]{:S(2)}) collective-permute-start(bf16[32,2176]{1,0:T(8,128)(2,1)S(1)} %get-tuple-element.27), channel_id=1, source_target_pairs={{0,2},{1,3},{2,0},{3,1},{4,6},{5,7},{6,4},{7,5},{8,10},{9,11},{10,... | collective-permute-start | bytes 417800 | tf_op jit(solution)/shard_map/ppermute | solution.py:433
  100.9 7.5 %collective-permute-start.6 = (bf16[32,2176]{1,0:T(8,128)(2,1)S(1)}, bf16[32,2176]{1,0:T(8,128)(2,1)S(1)}, u32[]{:S(2)}, u32[]{:S(2)}) collective-permute-start(bf16[32,2176]{1,0:T(8,128)(2,1)S(1)} %get-tuple-element.28), channel_id=1, source_target_pairs={{0,3},{1,2},{2,1},{3,0},{4,7},{5,6},{6,5},{7,4},{8,11},{9,10},{10,... | collective-permute-start | bytes 417800 | tf_op jit(solution)/shard_map/ppermute | solution.py:433

commit v3 on v2

--- a/solution.py
+++ b/solution.py
@@ -17,68 +17,46 @@
 LOG2E = math.log2(math.e)
 bf16, f32 = jnp.bfloat16, jnp.float32
 
-SIDES = 2
-
 
 def key_of(place):
-    half, side, ctx = place >> 10, (place >> 9) & 1, (place >> 4) & 31
-    return ctx * 64 + half * 32 + side * 16 + (place & 15)
-
-
-def lay_index_keys(keys, pieces, core):
-    count = pieces[0].shape[0]
-    for n, piece in enumerate(pieces):
-        spot = ((core ^ (n // SIDES)) * SIDES + n % SIDES) * count
-        keys[pl.ds(pl.multiple_of(spot, count), count), :] = piece[...]
-
-
-def index_key_specs(own):
-    first = own.shape[1] // IDX_DIM - SIDES
-    return [
-        pl.BlockSpec((own.shape[0], IDX_DIM), lambda g, where, at=first + side: (0, at))
-        for _ in range(2)
-        for side in range(SIDES)
-    ]
+    return ((place >> 5) & 31) * 64 + (place >> 10) * 32 + (place & 31)
+
+
+def lay_halves(keys, own, other, core, width):
+    half = own.shape[0]
+    keys[pl.ds(pl.multiple_of(core * half, half), half), 0:width] = own[...]
+    keys[pl.ds(pl.multiple_of((1 - core) * half, half), half), 0:width] = other[...]
 
 
 def head_kernel(where, q_hbm, own_hbm, other_hbm, *refs):
     outs, (keys, queries, pair, scores, probs, acc, turned, sems) = refs[:4], refs[4:]
     pairs, rows, both_width = queries.shape
     width = both_width // 2
-    count = own_hbm.shape[0]
-    n_keys = 2 * SIDES * count
+    half = own_hbm.shape[0]
+    n_keys = 2 * half
     wide = keys.shape[1] - rows
-    body = wide - rows
-
-    def key_copies(k, source):
-        for side in range(SIDES):
-            spot = ((where[0] ^ k) * SIDES + side) * count
-            at = pl.ds(pl.multiple_of(spot, count), count)
-            sem = (k * SIDES + side) * 2
-            yield pltpu.make_async_copy(
-                source.at[:, pl.ds(side * body, body)], keys.at[at, pl.ds(0, body)], sems.at[sem]
-            )
-            yield pltpu.make_async_copy(
-                source.at[:, pl.ds(SIDES * body, rows)],
-                keys.at[at, pl.ds(body, rows)],
-                sems.at[sem + 1],
-            )
+
+    def key_copy(k, source):
+        spot = pl.multiple_of((where[0] ^ k) * half, half)
+        return pltpu.make_async_copy(
+            source.at[:, pl.ds(0, wide)], keys.at[pl.ds(spot, half), pl.ds(0, wide)], sems.at[k]
+        )
 
     def query_copy(p):
         at = pl.multiple_of(p * both_width, 128)
         return pltpu.make_async_copy(
-            q_hbm.at[:, pl.ds(at, both_width)], queries.at[p], sems.at[8 + p]
+            q_hbm.at[:, pl.ds(at, both_width)], queries.at[p], sems.at[2 + p]
         )
 
-    for k, source in enumerate((own_hbm, other_hbm)):
-        for copy in key_copies(k, source):
-            copy.start()
+    key_copy(0, own_hbm).start()
     query_copy(0).start()
+    key_copy(1, other_hbm).start()
     for p in range(1, pairs):
         query_copy(p).start()
     place = lax.broadcasted_iota(jnp.int32, (n_keys, rows), 0)
     query = lax.broadcasted_iota(jnp.int32, (n_keys, rows), 1)
     keys[:, wide:] = jnp.where(key_of(place) > query + where[1], -1e30, 0.0).astype(bf16)
+    pair[:, width:wide] = jnp.zeros((2 * rows, wide - width), bf16)
     row = lax.broadcasted_iota(jnp.int32, (2 * rows, rows), 0)
     lane = lax.broadcasted_iota(jnp.int32, (2 * rows, rows), 1)
     pair[:, wide:] = jnp.where((row & (rows - 1)) == lane, 1.0, 0.0).astype(bf16)
@@ -86,50 +64,40 @@
     scale = MAIN_SCALE * LOG2E
     vec = (8, 2 * rows)
     tall = (n_keys // 8, 8, 2 * rows)
-    for k, source in enumerate((own_hbm, other_hbm)):
-        for copy in key_copies(k, source):
-            copy.wait()
-    lane = lax.broadcasted_iota(jnp.int32, (count, rows), 1)
-    for n in range(2 * SIDES):
-        at = slice(n * count, (n + 1) * count)
-        rest = keys[at, body:wide].astype(f32)
-        keys[at, body:wide] = jnp.where(lane // (wide - width) == n % SIDES, rest, 0.0).astype(bf16)
+    key_copy(0, own_hbm).wait()
+    key_copy(1, other_hbm).wait()
 
     def add_pair(recip):
         old = (probs[...].astype(f32).reshape(tall) * recip[None]).reshape(n_keys, 2 * rows)
         acc[...] += old[:, :rows] + old[:, rows:]
 
+    def exponentials(shift):
+        e = jnp.exp2(scores[...].reshape(tall) * scale - shift[None])
+        probs[...] = e.reshape(n_keys, 2 * rows).astype(bf16)
+        return jnp.broadcast_to(jnp.sum(jnp.sum(e, axis=0), axis=0, keepdims=True), vec)
+
     def step(p, carry):
         shift, recip = carry
-        last = jnp.minimum(p, pairs - 1)
-
-        @pl.when(p < pairs)
-        def _():
-            query_copy(p).wait()
-
-        both = queries[last]
-        for h in range(2):
-            at = slice(h * rows, (h + 1) * rows)
-            pair[at, 0:width] = both[:, h * width : (h + 1) * width]
-            pair[at, width:wide] = both[:, h * width + body : (h + 1) * width]
+        query_copy(p).wait()
+        both = queries[p]
+        pair[0:rows, 0:width] = both[:, :width]
+        pair[rows:, 0:width] = both[:, width:]
         add_pair(recip)
-        e = jnp.exp2(scores[...].reshape(tall) * scale - shift[None])
-        total = jnp.sum(e, axis=0)
-        probs[...] = e.reshape(n_keys, 2 * rows).astype(bf16)
+        total = exponentials(shift)
         new = lax.dot_general(
             keys[...], pair[...], (((1,), (1,)), ((), ())), preferred_element_type=f32
         )
         scores[...] = new
         top = jnp.max(new.reshape(tall), axis=0)
         top = jnp.broadcast_to(jnp.max(top, axis=0, keepdims=True), vec)
-        total = jnp.broadcast_to(jnp.sum(total, axis=0, keepdims=True), vec)
         return top * scale, jnp.where(p > 0, 1.0 / total, 0.0)
 
     scores[...] = jnp.zeros(scores.shape, f32)
     probs[...] = jnp.zeros(probs.shape, bf16)
     zero = jnp.zeros(vec, f32)
-    _, recip = lax.fori_loop(0, pairs + 1, step, (zero, zero))
+    shift, recip = lax.fori_loop(0, pairs, step, (zero, zero))
     add_pair(recip)
+    add_pair(1.0 / exponentials(shift))
     turned[...] = (acc[...] * (1.0 / 128.0)).T.astype(bf16)
     few = rows // 4
     for k in range(4):
@@ -138,7 +106,7 @@
 
 def head_totals(where, q, own, other):
     rows, columns = q.shape
-    n_keys = 2 * SIDES * own.shape[0]
+    n_keys = 2 * own.shape[0]
     pairs = columns // (2 * LATENT)
     vmem = pl.BlockSpec(memory_space=pltpu.VMEM)
     anywhere = pl.BlockSpec(memory_space=pl.ANY)
@@ -160,7 +128,7 @@
             pltpu.VMEM((n_keys, 2 * rows), bf16),
             pltpu.VMEM((n_keys, rows), f32),
             pltpu.VMEM((rows, n_keys), bf16),
-            pltpu.SemaphoreType.DMA((8 + pairs,)),
+            pltpu.SemaphoreType.DMA((2 + pairs,)),
         ],
         compiler_params=pltpu.CompilerParams(vmem_limit_bytes=56 * 2**20),
         cost_estimate=pl.CostEstimate(
@@ -176,14 +144,15 @@
 BIT = [1 << j for j in range(31)] + [-(2**31)]
 
 
-def forward_kernel(where, q_ref, w_ref, *refs):
-    pieces, (kl_ref, bits_ref, chance_ref, keys, block, logits) = refs[:4], refs[4:]
+def forward_kernel(
+    where, q_ref, w_ref, own_ref, other_ref, kl_ref, bits_ref, chance_ref, keys, block, logits
+):
     g = pl.program_id(0)
     rows, dim = q_ref.shape[0], keys.shape[1]
 
     @pl.when(g == 0)
     def _():
-        lay_index_keys(keys, pieces, where[0])
+        lay_halves(keys, own_ref, other_ref, where[0], dim)
         logits[...] = jnp.zeros(logits.shape, f32)
 
     for j in range(IDX_GROUP):
@@ -213,7 +182,7 @@
 
 def index_forward(where, q, w, own, other, kl):
     rows, dim = kl.shape[0], IDX_DIM
-    n_keys = 2 * SIDES * own.shape[0]
+    n_keys = 2 * own.shape[0]
     heads = q.shape[1] // dim
     wide = IDX_GROUP * dim
     return pl.pallas_call(
@@ -224,7 +193,8 @@
             in_specs=[
                 pl.BlockSpec((rows, wide), lambda g, where: (0, g)),
                 pl.BlockSpec((1, rows, IDX_GROUP), lambda g, where: (g, 0, 0)),
-                *index_key_specs(own),
+                pl.BlockSpec((n_keys // 2, dim), lambda g, where: (0, 5)),
+                pl.BlockSpec((n_keys // 2, dim), lambda g, where: (0, 5)),
                 pl.BlockSpec((rows, 1), lambda g, where: (0, 0)),
             ],
             out_specs=[
@@ -246,25 +216,25 @@
             flops=2 * heads * rows * n_keys * 256, bytes_accessed=10 * 2**20, transcendentals=2**16
         ),
         name="index_forward",
-    )(where, q, w, own, own, other, other, kl)
+    )(where, q, w, own, other, kl)
 
 
 def lay_masked(bits_ref, upstream, masked):
     rows = bits_ref.shape[0]
-    bits, up = bits_ref[...], upstream[...]
+    bits, up = bits_ref[...], upstream[...].astype(f32)
     for j in range(IDX_GROUP):
         masked[j * rows : (j + 1) * rows, :] = jnp.where(bits & BIT[j] != 0, up, 0.0).astype(bf16)
 
 
-def query_kernel(where, upstream_ref, bits_ref, q_ref, w_ref, *refs):
-    pieces, outs, (keys, masked, grad_ref) = refs[:4], refs[4:8], refs[8:]
+def query_kernel(where, upstream_ref, bits_ref, q_ref, w_ref, own_ref, other_ref, *refs):
+    outs, (keys, masked, grad_ref) = refs[:4], refs[4:]
     g = pl.program_id(0)
     rows, dim = q_ref.shape[0], keys.shape[1]
     wide = grad_ref.shape[2] - 128
 
     @pl.when(g == 0)
     def _():
-        lay_index_keys(keys, pieces, where[0])
+        lay_halves(keys, own_ref, other_ref, where[0], dim)
 
     lay_masked(bits_ref, upstream_ref, masked)
     plain = lax.dot_general(
@@ -300,7 +270,7 @@
         target = parts[0][...].astype(f32)
         for k in range(1, 4):
             target += parts[k][...].astype(f32)
-        upstream_ref[...] = chance_ref[...] - kl_ref[...] * target
+        upstream_ref[...] = (chance_ref[...] - kl_ref[...] * target).astype(bf16)
         acc[...] = jnp.zeros(acc.shape, f32)
 
     lay_masked(bits_ref, upstream_ref, masked)
@@ -315,9 +285,10 @@
     def _():
         for t in range(acc.shape[1] // 128):
             piece = (acc[:, t * 128 : (t + 1) * 128] * (dim ** (-0.5))).T.astype(bf16)
-            for b in range(0, 128, 16):
-                key = key_of(t * 128 + b)
-                gk_ref[key : key + 16, :] = piece[b : b + 16]
+            for b in range(4):
+                place = t * 128 + b * 32
+                key = ((place >> 5) & 31) * 64 + (place >> 10) * 32
+                gk_ref[key : key + 32, :] = piece[b * 32 : (b + 1) * 32]
 
 
 def whole(*shape):
@@ -339,7 +310,8 @@
                 pl.BlockSpec((rows, n_keys), lambda g, where: (g, 0)),
                 pl.BlockSpec((rows, IDX_GROUP * dim), lambda g, where: (0, g)),
                 pl.BlockSpec((1, rows, IDX_GROUP), lambda g, where: (g, 0, 0)),
-                *index_key_specs(own),
+                pl.BlockSpec((n_keys // 2, dim), lambda g, where: (0, 5)),
+                pl.BlockSpec((n_keys // 2, dim), lambda g, where: (0, 5)),
             ],
             out_specs=[whole(*out.shape)] * 4,
             scratch_shapes=[
@@ -354,7 +326,7 @@
             flops=4 * heads * rows * n_keys * 128, bytes_accessed=6 * 2**20, transcendentals=0
         ),
         name="index_query_grads",
-    )(where, upstream, bits, q, w, own, own, other, other)
+    )(where, upstream, bits, q, w, own, other)
 
 
 def index_key_grads(where, parts, chance, kl, bits, q, w):
@@ -382,7 +354,7 @@
         ),
         out_shape=[
             jax.ShapeDtypeStruct((n_keys, dim), bf16),
-            jax.ShapeDtypeStruct((rows, n_keys), f32),
+            jax.ShapeDtypeStruct((rows, n_keys), bf16),
         ],
         compiler_params=pltpu.CompilerParams(vmem_limit_bytes=24 * 2**20),
         cost_estimate=pl.CostEstimate(
@@ -444,13 +416,10 @@
     offset = query_start[0] + lax.axis_index(CTX) * rows - key_start[0]
     where = jnp.stack([core, offset, head]).astype(jnp.int32)
 
-    half, side = latents.shape[0] // 2, latents.shape[0] // 4
-    body = latents.shape[1] // 128 * 128
-    lat = lax.dynamic_slice_in_dim(latents, core * half, half, 0)
-    idx = lax.dynamic_slice_in_dim(idx_keys, core * half, half, 0)
-    parts = [lat[:, :body], lat[:, body:], idx]
-    slab = jnp.concatenate([p[at : at + side] for p in parts for at in (0, side)], axis=1)
-    own = to_all(slab, CTX).reshape(-1, slab.shape[1])
+    half = latents.shape[0] // 2
+    slab = jnp.concatenate([jnp.pad(latents, ((0, 0), (0, 64))), idx_keys], axis=1)
+    own = to_all(lax.dynamic_slice_in_dim(slab, core * half, half, 0), CTX)
+    own = own.reshape(-1, own.shape[-1])
     other = lax.ppermute(own, "core", [(0, 1), (1, 0)])
 
     kl = lax.dynamic_slice_in_dim(kl_cotangent, head * few, few, 0)[:, None]

time: 111 us -> 104 us (0.937)
  local copies, waits for them, and re-layouts: 13.2 us -> 1.59 us
  waiting for transfers between devices: 6.97 us -> 10.9 us
  blocking collectives: 28.7 us -> 30.2 us
    unnamed x32 -> x14, local copies, waits for them, and re-layouts: 6.49 us -> 1.07 us
    ppermute x6, waiting for transfers between devices: 6.96 us -> 9.86 us  [swap_heads(): lax.ppermute(pieces[k], HEAD, [(h, h ^ k) for h in range(count)])]
    slice x3 -> x0, local copies, waits for them, and re-layouts: 2.3 us -> none  [shards(): p[at:at + side]]
    all_to_all x1, blocking collectives: 28.7 us -> 30.2 us  [to_all(): return lax.all_to_all(copies, axes, split_axis=0, concat_axis=0, tiled=True)]
    dynamic_slice x1, local copies, waits for them, and re-layouts: 1.45 us -> 0.07 us  [shards(): w = lax.dynamic_slice_in_dim(idx_weight, head * few, few, 0)]
    reshape x1, local copies, waits for them, and re-layouts: 1.44 us -> 0.08 us  [shards(): w = w.reshape(few, -1, IDX_GROUP).transpose(1, 0, 2)]
    broadcast_in_dim x2, local copies, waits for them, and re-layouts: 1.32 us -> 0.17 us  [shards(): kl = lax.dynamic_slice_in_dim(kl_cotangent, head * few, few, 0)[:, None]]
  transfers between devices with their start and end apart: 8 -> 8, of which waited for: 3 -> 4; matrix products, arithmetic and copies ran while one was open for 4% -> 1% of each run, Pallas kernels for 9% -> 10%
where the time goes in v3:
time: 104 us; the launch traced here: 103 us
  Pallas kernels  40.4 us (39%)
  blocking collectives  30.2 us (29%)
  starting transfers between devices  16.6 us (16%)
  waiting for transfers between devices  10.9 us (10%)
  between operations  2.06 us (2%)
  other arithmetic  1.62 us (2%)
  local copies, waits for them, and re-layouts  1.59 us (2%)
    all_to_all x1, blocking collectives, to_all(): return lax.all_to_all(copies, axes, split_axis=0, concat_axis=0, tiled=True)  30.2 us
    pallas_call x1, Pallas kernels, head_totals(): pl.pallas_call(head_kernel, out_shape=[jax.ShapeDtypeStruct((rows // 4, n...  23.1 us
    ppermute x6, waiting for transfers between devices, swap_heads(): lax.ppermute(pieces[k], HEAD, [(h, h ^ k) for h in range(count)])  9.86 us
    ppermute x6, starting transfers between devices, swap_heads(): lax.ppermute(pieces[k], HEAD, [(h, h ^ k) for h in range(count)])  8.21 us
    all_to_all x1, starting transfers between devices, shards(): lax.all_to_all(gk.reshape(lax.axis_size(ALL), -1, gk.shape[1]), ALL, 0, 0...  5.93 us
    pallas_call x1, Pallas kernels, index_forward(): pl.pallas_call(forward_kernel, grid_spec=pltpu.PrefetchScalarGridSpec(num...  5.89 us
    pallas_call x1, Pallas kernels, index_key_grads(): pl.pallas_call(key_kernel, grid_spec=pltpu.PrefetchScalarGridSpec(num_sca...  5.34 us
    pallas_call x1, Pallas kernels, index_query_grads(): pl.pallas_call(query_kernel, grid_spec=pltpu.PrefetchScalarGridSpec(num_s...  4.44 us
  transfers between devices with their start and end apart: 8, of which 4 were waited for; matrix products, arithmetic and copies ran while one was open for 1% of the time, Pallas kernels for 10%

profile of v3, /device:TPU:1, one launch (start us, length us, event | category | flops | bytes accessed | tf_op | source)
XLA Modules:
  0.0 103.3 jit_solution(18437210134791698903)
XLA Ops:
  0.6 0.0 copy-start
  0.7 1.0 fusion.1
  1.6 0.0 copy-start.6
  1.6 0.0 copy-start.5
  1.6 0.2 broadcast_in_dim.6
  1.8 30.2 %all_to_all.10 = bf16[32,32,768]{2,1,0:T(8,128)(2,1)} all-to-all(bf16[32,32,768]{2,1,0:T(8,128)(2,1)S(1)} %broadcast_in_dim.6), channel_id=1, replica_groups=mesh['ctx_0'=2,'ctx_1'=4,'ctx_2'=4,'far'=2,'core'=2] {'ctx_0','ctx_1','c..., dimensions={0} | all-to-all | bytes 3145728 | tf_op jit(solution)/shard_map/all_to_all | solution.py:369
  32.0 2.4 %collective-permute-start = (bf16[1024,768]{1,0:T(8,128)(2,1)}, bf16[1024,768]{1,0:T(8,128)(2,1)}, u32[]{:S(2)}, u32[]{:S(2)}) collective-permute-start(bf16[1024,768]{1,0:T(8,128)(2,1)} %bitcast.5.own_hbm.own_ref), channel_id=1, source_target_pairs={{0,1},{1,0},{2,3},{3,2},{4,5},{5,4},{6,7},{7,6},{8,9},{9,8},{10,11... | collective-permute-start | bytes 4718600 | tf_op jit(solution)/shard_map/ppermute | solution.py:423
  35.7 0.0 copy-done.6
  35.7 0.1 dynamic-slice_bitcast_fusion
  35.8 0.1 copy.15.kl_ref.refs_5_
  35.9 0.0 copy-done.5
  35.9 0.1 constant_dynamic-slice_fusion
  36.0 0.1 copy.14
  36.0 0.7 pad_add_fusion.where
  36.7 0.0 copy-done
  36.8 0.0 copy-start.1
  36.8 1.0 collective-permute-done.other_hbm.other_ref
  37.8 23.1 %head_totals.1 = (bf16[32,2048]{1,0:T(8,128)(2,1)}, bf16[32,2048]{1,0:T(8,128)(2,1)}, bf16[32,2048]{1,0:T(8,128)(2,1)}, bf16[32,2048]{1,0:T(8,128)(2,1)}) custom-call(s32[3]{0:T(128)} %pad_add_fusion.where, bf16[128,18432]{1,0:T(8,128)(2,1)} %q_hbm.1, bf16[1024,768]{1,0:T(8,128)(2,1)} %bitcast.5.own_hbm.own_ref, ...), custom_call_target="tpu_custom_call" | custom-call | flops 12884901888 | bytes 8388608 | tf_op jit(solution)/shard_map/head_totals/pallas_call | solution.py:113
  60.9 0.5 collective-permute-start.1
  61.4 3.3 %collective-permute-start.2 = (bf16[32,2048]{1,0:T(8,128)(2,1)}, bf16[32,2048]{1,0:T(8,128)(2,1)S(1)}, u32[]{:S(2)}, u32[]{:S(2)}) collective-permute-start(bf16[32,2048]{1,0:T(8,128)(2,1)} %get-tuple-element.20), channel_id=1, source_target_pairs={{0,2},{1,3},{2,0},{3,1},{4,6},{5,7},{6,4},{7,5},{8,10},{9,11},{10,... | collective-permute-start | bytes 393224 | tf_op jit(solution)/shard_map/ppermute | solution.py:405
  64.7 0.1 collective-permute-start.3
  64.8 0.0 copy-done.1
  64.8 0.0 copy-start.4
  64.8 5.9 %index_forward.1 = (s32[64,2048]{1,0:T(8,128)S(1)}, f32[32,2048]{1,0:T(8,128)S(1)}) custom-call(s32[3]{0:T(128)S(1)} %copy-done.1, bf16[32,8192]{1,0:T(8,128)(2,1)S(1)} %constant_dynamic-slice_fusion.1.q_ref.refs_7_, f32[2,32,32]{2,1,0:T(8,128)S(1)} %bitcast.14, bf16[1024,768]{1,0:T(8,128)(2,1)} %bitcast.5.own_hbm.own_ref, ...), custom_call_target="tpu_custom_call" | custom-call | flops 2147483648 | bytes 10485760 | tf_op jit(solution)/shard_map/index_forward/pallas_call | solution.py:188
  70.7 0.0 copy-start.2
  70.7 0.0 collective-permute-done.1.refs_1_
  70.7 0.0 collective-permute-done.2.refs_2_
  70.7 1.3 %collective-permute-done.3.refs_3_ = bf16[32,2048]{1,0:T(8,128)(2,1)S(1)} collective-permute-done((bf16[32,2048]{1,0:T(8,128)(2,1)}, bf16[32,2048]{1,0:T(8,128)(2,1)S(1)}, u32[]{:S(2)}, u32[]{:S(2)}) %collective-permute-start.3) | collective-permute-done | bytes 131104 | tf_op jit(solution)/shard_map/ppermute | solution.py:405
  72.0 0.0 copy-done.4
  72.0 5.3 %index_key_grads.1 = (bf16[2048,128]{1,0:T(8,128)(2,1)}, bf16[32,2048]{1,0:T(8,128)(2,1)S(1)}) custom-call(s32[3]{0:T(128)S(1)} %copy-done.1, bf16[32,2048]{1,0:T(8,128)(2,1)S(1)} %copy-done.4, bf16[32,2048]{1,0:T(8,128)(2,1)S(1)} %collective-permute-done.1.refs_1_, bf16[32,2048]{1,0:T(8,128)(2,1)S(1)} %collective-permute-done.2.refs_2_, ...), custom_call_target="tpu_custom_call" | custom-call | flops 2147483648 | bytes 6291456 | tf_op jit(solution)/shard_map/index_key_grads/pallas_call | solution.py:336
  77.3 0.0 copy-done.2
  77.3 5.9 %all-to-all-start.1 = ((bf16[128,16,128]{2,1,0:T(8,128)(2,1)}), bf16[128,16,128]{2,1,0:T(8,128)(2,1)S(1)}, u32[]{:S(2)}, u32[]{:S(2)}) async-start(bf16[128,16,128]{2,1,0:T(8,128)(2,1)} %bitcast.9), calls=%async_computation.1 | async-start | bytes 1048576 | tf_op jit(solution)/shard_map/all_to_all | solution.py:434
  83.3 0.0 copy-start.3
  83.3 1.0 copy-done.3
  84.3 4.4 %index_query_grads.1 = (bf16[32,2176]{1,0:T(8,128)(2,1)S(1)}, bf16[32,2176]{1,0:T(8,128)(2,1)S(1)}, bf16[32,2176]{1,0:T(8,128)(2,1)S(1)}, bf16[32,2176]{1,0:T(8,128)(2,1)S(1)}) custom-call(s32[3]{0:T(128)S(1)} %copy-done.1, bf16[32,2048]{1,0:T(8,128)(2,1)S(1)} %get-tuple-element.24.upstream_ref, s32[64,2048]{1,0:T(8,128)S(1)} %copy-done.3, ...), custom_call_target="tpu_custom_call" | custom-call | flops 2147483648 | bytes 6291456 | tf_op jit(solution)/shard_map/index_query_grads/pallas_call | solution.py:303
  88.8 1.1 %collective-permute-start.4 = (bf16[32,2176]{1,0:T(8,128)(2,1)S(1)}, bf16[32,2176]{1,0:T(8,128)(2,1)S(1)}, u32[]{:S(2)}, u32[]{:S(2)}) collective-permute-start(bf16[32,2176]{1,0:T(8,128)(2,1)S(1)} %get-tuple-element.26), channel_id=1, source_target_pairs={{0,1},{1,0},{2,3},{3,2},{4,5},{5,4},{6,7},{7,6},{8,9},{9,8},{10,11... | collective-permute-start | bytes 417800 | tf_op jit(solution)/shard_map/ppermute | solution.py:405
  89.9 2.6 %collective-permute-start.5 = (bf16[32,2176]{1,0:T(8,128)(2,1)S(1)}, bf16[32,2176]{1,0:T(8,128)(2,1)S(1)}, u32[]{:S(2)}, u32[]{:S(2)}) collective-permute-start(bf16[32,2176]{1,0:T(8,128)(2,1)S(1)} %get-tuple-element.27), channel_id=1, source_target_pairs={{0,2},{1,3},{2,0},{3,1},{4,6},{5,7},{6,4},{7,5},{8,10},{9,11},{10,... | collective-permute-start | bytes 417800 | tf_op jit(solution)/shard_map/ppermute | solution.py:405
  92.5 0.7 collective-permute-start.6
  93.2 0.0 collective-permute-done.4.refs_1_
  93.2 5.6 %collective-permute-done.5.refs_2_ = bf16[32,2176]{1,0:T(8,128)(2,1)S(1)} collective-permute-done((bf16[32,2176]{1,0:T(8,128)(2,1)S(1)}, bf16[32,2176]{1,0:T(8,128)(2,1)S(1)}, u32[]{:S(2)}, u32[]{:S(2)}) %collective-permute-start.5) | collective-permute-done | bytes 139296 | tf_op jit(solution)/shard_map/ppermute | solution.py:405
  98.7 3.0 %collective-permute-done.6.refs_3_ = bf16[32,2176]{1,0:T(8,128)(2,1)S(1)} collective-permute-done((bf16[32,2176]{1,0:T(8,128)(2,1)S(1)}, bf16[32,2176]{1,0:T(8,128)(2,1)S(1)}, u32[]{:S(2)}, u32[]{:S(2)}) %collective-permute-start.6) | collective-permute-done | bytes 139296 | tf_op jit(solution)/shard_map/ppermute | solution.py:405
  101.7 0.0 all-to-all-done.1.refs_4_
  101.7 1.6 %finish.1 = (f32[128,2048]{1,0:T(8,128)}, f32[16,128]{1,0:T(8,128)}, f32[16,128]{1,0:T(8,128)}) custom-call(s32[3]{0:T(128)S(1)} %copy-done.1, bf16[32,2176]{1,0:T(8,128)(2,1)S(1)} %get-tuple-element.25.refs_0_, bf16[32,2176]{1,0:T(8,128)(2,1)S(1)} %collective-permute-done.4.refs_1_, bf16[32,2176]{1,0:T(8,128)(2,1)S(1)} %collective-permute-done.5.refs_2_, ...), custom_call_target="tpu_custom_call" | custom-call | flops 1048576 | bytes 2097152 | tf_op jit(solution)/shard_map/finish/pallas_call | solution.py:386
  (1 shorter events, 0.0 us)
Async XLA Ops:
  0.6 36.1 %copy-start = (bf16[128,8192]{1,0:T(8,128)(2,1)S(1)}, bf16[128,8192]{1,0:T(8,128)(2,1)}, u32[]{:S(2)}) copy-start(bf16[128,8192]{1,0:T(8,128)(2,1)} %param.10) | copy-start | bytes 6291460
  1.6 34.1 %copy-start.6 = (f32[128]{0:T(128)S(1)}, f32[128]{0:T(128)}, u32[]{:S(2)}) copy-start(f32[128]{0:T(128)} %param.13) | copy-start | bytes 1540
  1.6 34.3 %copy-start.5 = (f32[128,64]{0,1:T(8,128)S(1)}, f32[128,64]{0,1:T(8,128)}, u32[]{:S(2)}) copy-start(f32[128,64]{0,1:T(8,128)} %param.11) | copy-start | bytes 98308
  32.0 5.8 %collective-permute-start = (bf16[1024,768]{1,0:T(8,128)(2,1)}, bf16[1024,768]{1,0:T(8,128)(2,1)}, u32[]{:S(2)}, u32[]{:S(2)}) collective-permute-start(bf16[1024,768]{1,0:T(8,128)(2,1)} %bitcast.5.own_hbm.own_ref), channel_id=1, source_target_pairs={{0,1},{1,0},{2,3},{3,2},{4,5},{5,4},{6,7},{7,6},{8,9},{9,8},{10,11... | collective-permute-start | bytes 4718600 | tf_op jit(solution)/shard_map/ppermute | solution.py:423
  36.8 28.0 %copy-start.1 = (s32[3]{0:T(128)S(1)}, s32[3]{0:T(128)}, u32[]{:S(2)}) copy-start(s32[3]{0:T(128)} %pad_add_fusion.where) | copy-start | bytes 40
  60.9 9.8 %collective-permute-start.1 = (bf16[32,2048]{1,0:T(8,128)(2,1)}, bf16[32,2048]{1,0:T(8,128)(2,1)S(1)}, u32[]{:S(2)}, u32[]{:S(2)}) collective-permute-start(bf16[32,2048]{1,0:T(8,128)(2,1)} %get-tuple-element.19), channel_id=1, source_target_pairs={{0,1},{1,0},{2,3},{3,2},{4,5},{5,4},{6,7},{7,6},{8,9},{9,8},{10,11... | collective-permute-start | bytes 393224 | tf_op jit(solution)/shard_map/ppermute | solution.py:405
  61.4 9.3 %collective-permute-start.2 = (bf16[32,2048]{1,0:T(8,128)(2,1)}, bf16[32,2048]{1,0:T(8,128)(2,1)S(1)}, u32[]{:S(2)}, u32[]{:S(2)}) collective-permute-start(bf16[32,2048]{1,0:T(8,128)(2,1)} %get-tuple-element.20), channel_id=1, source_target_pairs={{0,2},{1,3},{2,0},{3,1},{4,6},{5,7},{6,4},{7,5},{8,10},{9,11},{10,... | collective-permute-start | bytes 393224 | tf_op jit(solution)/shard_map/ppermute | solution.py:405
  64.7 7.3 %collective-permute-start.3 = (bf16[32,2048]{1,0:T(8,128)(2,1)}, bf16[32,2048]{1,0:T(8,128)(2,1)S(1)}, u32[]{:S(2)}, u32[]{:S(2)}) collective-permute-start(bf16[32,2048]{1,0:T(8,128)(2,1)} %get-tuple-element.21), channel_id=1, source_target_pairs={{0,3},{1,2},{2,1},{3,0},{4,7},{5,6},{6,5},{7,4},{8,11},{9,10},{10,... | collective-permute-start | bytes 393224 | tf_op jit(solution)/shard_map/ppermute | solution.py:405
  64.8 7.2 %copy-start.4 = (bf16[32,2048]{1,0:T(8,128)(2,1)S(1)}, bf16[32,2048]{1,0:T(8,128)(2,1)}, u32[]{:S(2)}) copy-start(bf16[32,2048]{1,0:T(8,128)(2,1)} %get-tuple-element.18.refs_0_) | copy-start | bytes 393220
  70.7 6.7 %copy-start.2 = (s32[64,2048]{1,0:T(8,128)}, s32[64,2048]{1,0:T(8,128)S(1)}, u32[]{:S(2)}) copy-start(s32[64,2048]{1,0:T(8,128)S(1)} %get-tuple-element.23.refs_6_.bits_ref) | copy-start | bytes 1572868
  77.3 24.4 %all-to-all-start.1 = ((bf16[128,16,128]{2,1,0:T(8,128)(2,1)}), bf16[128,16,128]{2,1,0:T(8,128)(2,1)S(1)}, u32[]{:S(2)}, u32[]{:S(2)}) async-start(bf16[128,16,128]{2,1,0:T(8,128)(2,1)} %bitcast.9), calls=%async_computation.1 | async-start | bytes 1048576 | tf_op jit(solution)/shard_map/all_to_all | solution.py:434
  83.3 1.0 %copy-start.3 = (s32[64,2048]{1,0:T(8,128)S(1)}, s32[64,2048]{1,0:T(8,128)}, u32[]{:S(2)}) copy-start(s32[64,2048]{1,0:T(8,128)} %copy-done.2) | copy-start | bytes 1572868
  88.8 4.4 %collective-permute-start.4 = (bf16[32,2176]{1,0:T(8,128)(2,1)S(1)}, bf16[32,2176]{1,0:T(8,128)(2,1)S(1)}, u32[]{:S(2)}, u32[]{:S(2)}) collective-permute-start(bf16[32,2176]{1,0:T(8,128)(2,1)S(1)} %get-tuple-element.26), channel_id=1, source_target_pairs={{0,1},{1,0},{2,3},{3,2},{4,5},{5,4},{6,7},{7,6},{8,9},{9,8},{10,11... | collective-permute-start | bytes 417800 | tf_op jit(solution)/shard_map/ppermute | solution.py:405
  89.9 8.8 %collective-permute-start.5 = (bf16[32,2176]{1,0:T(8,128)(2,1)S(1)}, bf16[32,2176]{1,0:T(8,128)(2,1)S(1)}, u32[]{:S(2)}, u32[]{:S(2)}) collective-permute-start(bf16[32,2176]{1,0:T(8,128)(2,1)S(1)} %get-tuple-element.27), channel_id=1, source_target_pairs={{0,2},{1,3},{2,0},{3,1},{4,6},{5,7},{6,4},{7,5},{8,10},{9,11},{10,... | collective-permute-start | bytes 417800 | tf_op jit(solution)/shard_map/ppermute | solution.py:405
  92.5 9.2 %collective-permute-start.6 = (bf16[32,2176]{1,0:T(8,128)(2,1)S(1)}, bf16[32,2176]{1,0:T(8,128)(2,1)S(1)}, u32[]{:S(2)}, u32[]{:S(2)}) collective-permute-start(bf16[32,2176]{1,0:T(8,128)(2,1)S(1)} %get-tuple-element.28), channel_id=1, source_target_pairs={{0,3},{1,2},{2,1},{3,0},{4,7},{5,6},{6,5},{7,4},{8,11},{9,10},{10,... | collective-permute-start | bytes 417800 | tf_op jit(solution)/shard_map/ppermute | solution.py:405

commit v4 on v3

--- a/solution.py
+++ b/solution.py
@@ -144,9 +144,8 @@
 BIT = [1 << j for j in range(31)] + [-(2**31)]
 
 
-def forward_kernel(
-    where, q_ref, w_ref, own_ref, other_ref, kl_ref, bits_ref, chance_ref, keys, block, logits
-):
+def forward_kernel(where, q_ref, w_ref, own_ref, other_ref, kl_ref, *refs):
+    bits_ref, chance_ref, gained_ref, keys, block, gained, logits = refs
     g = pl.program_id(0)
     rows, dim = q_ref.shape[0], keys.shape[1]
 
@@ -156,7 +155,10 @@
         logits[...] = jnp.zeros(logits.shape, f32)
 
     for j in range(IDX_GROUP):
-        block[j * rows : (j + 1) * rows, :] = q_ref[:, j * dim : (j + 1) * dim]
+        at = slice(j * rows, (j + 1) * rows)
+        block[at, :] = q_ref[:, j * dim : (j + 1) * dim]
+        gained[at, :] = q_ref[:, j * dim : (j + 1) * dim].astype(f32) * w_ref[0, :, j : j + 1]
+    gained_ref[...] = gained[...].T.astype(bf16)
     inner = lax.dot_general(
         block[...], keys[...], (((1,), (1,)), ((), ())), preferred_element_type=f32
     )
@@ -200,16 +202,19 @@
             out_specs=[
                 pl.BlockSpec((rows, n_keys), lambda g, where: (g, 0)),
                 pl.BlockSpec((rows, n_keys), lambda g, where: (0, 0)),
+                pl.BlockSpec((dim, IDX_GROUP * rows), lambda g, where: (0, g)),
             ],
             scratch_shapes=[
                 pltpu.VMEM((n_keys, dim), bf16),
                 pltpu.VMEM((IDX_GROUP * rows, dim), bf16),
+                pltpu.VMEM((IDX_GROUP * rows, dim), f32),
                 pltpu.VMEM((rows, n_keys), f32),
             ],
         ),
         out_shape=[
             jax.ShapeDtypeStruct((heads // IDX_GROUP * rows, n_keys), jnp.int32),
             jax.ShapeDtypeStruct((rows, n_keys), f32),
+            jax.ShapeDtypeStruct((dim, heads * rows), bf16),
         ],
         compiler_params=pltpu.CompilerParams(vmem_limit_bytes=24 * 2**20),
         cost_estimate=pl.CostEstimate(
@@ -261,9 +266,9 @@
 
 def key_kernel(where, *refs):
     parts, refs = refs[:4], refs[4:]
-    chance_ref, kl_ref, bits_ref, q_ref, w_ref, gk_ref, upstream_ref, masked, block, acc = refs
+    chance_ref, kl_ref, bits_ref, gained_ref, gk_ref, upstream_ref, masked, acc = refs
     g = pl.program_id(0)
-    rows, dim = q_ref.shape[0], block.shape[1]
+    dim = acc.shape[0]
 
     @pl.when(g == 0)
     def _():
@@ -274,11 +279,8 @@
         acc[...] = jnp.zeros(acc.shape, f32)
 
     lay_masked(bits_ref, upstream_ref, masked)
-    for j in range(IDX_GROUP):
-        q = q_ref[:, j * dim : (j + 1) * dim].astype(f32)
-        block[j * rows : (j + 1) * rows, :] = (q * w_ref[0, :, j : j + 1]).astype(bf16)
     acc[...] += lax.dot_general(
-        block[...], masked[...], (((0,), (0,)), ((), ())), preferred_element_type=f32
+        gained_ref[...], masked[...], (((1,), (0,)), ((), ())), preferred_element_type=f32
     )
 
     @pl.when(g == pl.num_programs(0) - 1)
@@ -329,10 +331,10 @@
     )(where, upstream, bits, q, w, own, other)
 
 
-def index_key_grads(where, parts, chance, kl, bits, q, w):
+def index_key_grads(where, parts, chance, kl, bits, gained):
     rows, n_keys = chance.shape
     dim = IDX_DIM
-    heads = q.shape[1] // dim
+    heads = gained.shape[1] // rows
     return pl.pallas_call(
         key_kernel,
         grid_spec=pltpu.PrefetchScalarGridSpec(
@@ -342,13 +344,11 @@
                 *[whole(rows, n_keys)] * 5,
                 whole(rows, 1),
                 pl.BlockSpec((rows, n_keys), lambda g, where: (g, 0)),
-                pl.BlockSpec((rows, IDX_GROUP * dim), lambda g, where: (0, g)),
-                pl.BlockSpec((1, rows, IDX_GROUP), lambda g, where: (g, 0, 0)),
+                pl.BlockSpec((dim, IDX_GROUP * rows), lambda g, where: (0, g)),
             ],
             out_specs=[whole(n_keys, dim), whole(rows, n_keys)],
             scratch_shapes=[
                 pltpu.VMEM((IDX_GROUP * rows, n_keys), bf16),
-                pltpu.VMEM((IDX_GROUP * rows, dim), bf16),
                 pltpu.VMEM((dim, n_keys), f32),
             ],
         ),
@@ -361,7 +361,7 @@
             flops=4 * heads * rows * n_keys * 128, bytes_accessed=6 * 2**20, transcendentals=0
         ),
         name="index_key_grads",
-    )(where, *parts, chance, kl, bits, q, w)
+    )(where, *parts, chance, kl, bits, gained)
 
 
 def to_all(piece, axes):
@@ -429,8 +429,8 @@
     few_queries = lax.dynamic_slice_in_dim(idx_query, head * few, few, 0)
 
     parts = swap_heads(head_totals(where, main_query, own, other))
-    bits, chance = index_forward(where, few_queries, w, own, other, kl)
-    gk, upstream = index_key_grads(where, parts, chance, kl, bits, few_queries, w)
+    bits, chance, gained = index_forward(where, few_queries, w, own, other, kl)
+    gk, upstream = index_key_grads(where, parts, chance, kl, bits, gained)
     pieces = lax.all_to_all(gk.reshape(lax.axis_size(ALL), -1, gk.shape[1]), ALL, 0, 0, tiled=True)
     grads = index_query_grads(where, upstream, bits, few_queries, w, own, other)
     grad_query, grad_weight, grad_keys = finish(where, swap_heads(grads), pieces)

time: 104 us -> 102 us (0.981)
  Pallas kernels: 40.4 us -> 38.8 us
    pallas_call x1, Pallas kernels: 5.34 us -> 3.37 us  [index_key_grads(): pl.pallas_call(key_kernel, grid_spec=pltpu.PrefetchScalarGridSpec(num_sca...]
  transfers between devices with their start and end apart: 8 -> 8, of which waited for: 4 -> 4; matrix products, arithmetic and copies ran while one was open for 1% -> 1% of each run, Pallas kernels for 10% -> 11%
where the time goes in v4:
time: 102 us; the launch traced here: 101 us
  Pallas kernels  38.8 us (38%)
  blocking collectives  30.2 us (30%)
  starting transfers between devices  16.6 us (16%)
  waiting for transfers between devices  10.5 us (10%)
  between operations  2.06 us (2%)
  other arithmetic  1.62 us (2%)
  local copies, waits for them, and re-layouts  1.59 us (2%)
    all_to_all x1, blocking collectives, to_all(): return lax.all_to_all(copies, axes, split_axis=0, concat_axis=0, tiled=True)  30.2 us
    pallas_call x1, Pallas kernels, head_totals(): pl.pallas_call(head_kernel, out_shape=[jax.ShapeDtypeStruct((rows // 4, n...  23.1 us
    ppermute x6, waiting for transfers between devices, swap_heads(): lax.ppermute(pieces[k], HEAD, [(h, h ^ k) for h in range(count)])  9.51 us
    ppermute x6, starting transfers between devices, swap_heads(): lax.ppermute(pieces[k], HEAD, [(h, h ^ k) for h in range(count)])  8.21 us
    pallas_call x1, Pallas kernels, index_forward(): pl.pallas_call(forward_kernel, grid_spec=pltpu.PrefetchScalarGridSpec(num...  6.24 us
    all_to_all x1, starting transfers between devices, shards(): lax.all_to_all(gk.reshape(lax.axis_size(ALL), -1, gk.shape[1]), ALL, 0, 0...  5.93 us
    pallas_call x1, Pallas kernels, index_query_grads(): pl.pallas_call(query_kernel, grid_spec=pltpu.PrefetchScalarGridSpec(num_s...  4.44 us
    pallas_call x1, Pallas kernels, index_key_grads(): pl.pallas_call(key_kernel, grid_spec=pltpu.PrefetchScalarGridSpec(num_sca...  3.37 us
  transfers between devices with their start and end apart: 8, of which 4 were waited for; matrix products, arithmetic and copies ran while one was open for 1% of the time, Pallas kernels for 11%

profile of v4, /device:TPU:1, one launch (start us, length us, event | category | flops | bytes accessed | tf_op | source)
XLA Modules:
  0.0 101.3 jit_solution(12185918688697130922)
XLA Ops:
  0.6 0.0 copy-start
  0.7 1.0 fusion.1
  1.6 0.0 copy-start.6
  1.6 0.0 copy-start.5
  1.6 0.2 broadcast_in_dim.6
  1.8 30.2 %all_to_all.10 = bf16[32,32,768]{2,1,0:T(8,128)(2,1)} all-to-all(bf16[32,32,768]{2,1,0:T(8,128)(2,1)S(1)} %broadcast_in_dim.6), channel_id=1, replica_groups=mesh['ctx_0'=2,'ctx_1'=4,'ctx_2'=4,'far'=2,'core'=2] {'ctx_0','ctx_1','c..., dimensions={0} | all-to-all | bytes 3145728 | tf_op jit(solution)/shard_map/all_to_all | solution.py:369
  32.0 2.4 %collective-permute-start = (bf16[1024,768]{1,0:T(8,128)(2,1)}, bf16[1024,768]{1,0:T(8,128)(2,1)}, u32[]{:S(2)}, u32[]{:S(2)}) collective-permute-start(bf16[1024,768]{1,0:T(8,128)(2,1)} %bitcast.5.own_hbm.own_ref), channel_id=1, source_target_pairs={{0,1},{1,0},{2,3},{3,2},{4,5},{5,4},{6,7},{7,6},{8,9},{9,8},{10,11... | collective-permute-start | bytes 4718600 | tf_op jit(solution)/shard_map/ppermute | solution.py:423
  35.7 0.0 copy-done.6
  35.7 0.1 dynamic-slice_bitcast_fusion
  35.8 0.1 copy.15.kl_ref.refs_5_
  35.9 0.0 copy-done.5
  35.9 0.1 constant_dynamic-slice_fusion
  36.0 0.1 copy.14
  36.0 0.7 pad_add_fusion.where
  36.7 0.0 copy-done
  36.8 0.0 copy-start.1
  36.8 1.0 %collective-permute-done.other_hbm.other_ref = bf16[1024,768]{1,0:T(8,128)(2,1)} collective-permute-done((bf16[1024,768]{1,0:T(8,128)(2,1)}, bf16[1024,768]{1,0:T(8,128)(2,1)}, u32[]{:S(2)}, u32[]{:S(2)}) %collective-permute-start) | collective-permute-done | bytes 1572896 | tf_op jit(solution)/shard_map/ppermute | solution.py:423
  37.8 23.1 %head_totals.1 = (bf16[32,2048]{1,0:T(8,128)(2,1)}, bf16[32,2048]{1,0:T(8,128)(2,1)}, bf16[32,2048]{1,0:T(8,128)(2,1)}, bf16[32,2048]{1,0:T(8,128)(2,1)}) custom-call(s32[3]{0:T(128)} %pad_add_fusion.where, bf16[128,18432]{1,0:T(8,128)(2,1)} %q_hbm.1, bf16[1024,768]{1,0:T(8,128)(2,1)} %bitcast.5.own_hbm.own_ref, ...), custom_call_target="tpu_custom_call" | custom-call | flops 12884901888 | bytes 8388608 | tf_op jit(solution)/shard_map/head_totals/pallas_call | solution.py:113
  60.9 0.5 collective-permute-start.1
  61.4 3.3 %collective-permute-start.2 = (bf16[32,2048]{1,0:T(8,128)(2,1)}, bf16[32,2048]{1,0:T(8,128)(2,1)S(1)}, u32[]{:S(2)}, u32[]{:S(2)}) collective-permute-start(bf16[32,2048]{1,0:T(8,128)(2,1)} %get-tuple-element.21), channel_id=1, source_target_pairs={{0,2},{1,3},{2,0},{3,1},{4,6},{5,7},{6,4},{7,5},{8,10},{9,11},{10,... | collective-permute-start | bytes 393224 | tf_op jit(solution)/shard_map/ppermute | solution.py:405
  64.7 0.1 collective-permute-start.3
  64.8 0.0 copy-done.1
  64.8 0.0 copy-start.4
  64.8 6.2 %index_forward.1 = (s32[64,2048]{1,0:T(8,128)S(1)}, f32[32,2048]{1,0:T(8,128)S(1)}, bf16[128,2048]{1,0:T(8,128)(2,1)S(1)}) custom-call(s32[3]{0:T(128)S(1)} %copy-done.1, bf16[32,8192]{1,0:T(8,128)(2,1)S(1)} %constant_dynamic-slice_fusion.1.q_ref, f32[2,32,32]{2,1,0:T(8,128)S(1)} %bitcast.14, bf16[1024,768]{1,0:T(8,128)(2,1)} %bitcast.5.own_hbm.own_ref, ...), custom_call_target="tpu_custom_call" | custom-call | flops 2147483648 | bytes 10485760 | tf_op jit(solution)/shard_map/index_forward/pallas_call | solution.py:190
  71.0 0.0 copy-start.2
  71.0 0.0 collective-permute-done.1.refs_1_
  71.0 0.0 collective-permute-done.2.refs_2_
  71.0 1.0 collective-permute-done.3.refs_3_
  72.0 0.0 copy-done.4
  72.0 3.4 %index_key_grads.1 = (bf16[2048,128]{1,0:T(8,128)(2,1)}, bf16[32,2048]{1,0:T(8,128)(2,1)S(1)}) custom-call(s32[3]{0:T(128)S(1)} %copy-done.1, bf16[32,2048]{1,0:T(8,128)(2,1)S(1)} %copy-done.4, bf16[32,2048]{1,0:T(8,128)(2,1)S(1)} %collective-permute-done.1.refs_1_, bf16[32,2048]{1,0:T(8,128)(2,1)S(1)} %collective-permute-done.2.refs_2_, ...), custom_call_target="tpu_custom_call" | custom-call | flops 2147483648 | bytes 6291456 | tf_op jit(solution)/shard_map/index_key_grads/pallas_call | solution.py:338
  75.4 0.0 copy-done.2
  75.4 5.9 %all-to-all-start.1 = ((bf16[128,16,128]{2,1,0:T(8,128)(2,1)}), bf16[128,16,128]{2,1,0:T(8,128)(2,1)S(1)}, u32[]{:S(2)}, u32[]{:S(2)}) async-start(bf16[128,16,128]{2,1,0:T(8,128)(2,1)} %bitcast.9), calls=%async_computation.1 | async-start | bytes 1048576 | tf_op jit(solution)/shard_map/all_to_all | solution.py:434
  81.3 0.0 copy-start.3
  81.3 1.0 %copy-done.3 = s32[64,2048]{1,0:T(8,128)S(1)} copy-done((s32[64,2048]{1,0:T(8,128)S(1)}, s32[64,2048]{1,0:T(8,128)}, u32[]{:S(2)}) %copy-start.3) | copy-done | bytes 524312
  82.4 4.4 %index_query_grads.1 = (bf16[32,2176]{1,0:T(8,128)(2,1)S(1)}, bf16[32,2176]{1,0:T(8,128)(2,1)S(1)}, bf16[32,2176]{1,0:T(8,128)(2,1)S(1)}, bf16[32,2176]{1,0:T(8,128)(2,1)S(1)}) custom-call(s32[3]{0:T(128)S(1)} %copy-done.1, bf16[32,2048]{1,0:T(8,128)(2,1)S(1)} %get-tuple-element.26.upstream_ref, s32[64,2048]{1,0:T(8,128)S(1)} %copy-done.3, ...), custom_call_target="tpu_custom_call" | custom-call | flops 2147483648 | bytes 6291456 | tf_op jit(solution)/shard_map/index_query_grads/pallas_call | solution.py:305
  86.8 1.1 %collective-permute-start.4 = (bf16[32,2176]{1,0:T(8,128)(2,1)S(1)}, bf16[32,2176]{1,0:T(8,128)(2,1)S(1)}, u32[]{:S(2)}, u32[]{:S(2)}) collective-permute-start(bf16[32,2176]{1,0:T(8,128)(2,1)S(1)} %get-tuple-element.28), channel_id=1, source_target_pairs={{0,1},{1,0},{2,3},{3,2},{4,5},{5,4},{6,7},{7,6},{8,9},{9,8},{10,11... | collective-permute-start | bytes 417800 | tf_op jit(solution)/shard_map/ppermute | solution.py:405
  88.0 2.6 %collective-permute-start.5 = (bf16[32,2176]{1,0:T(8,128)(2,1)S(1)}, bf16[32,2176]{1,0:T(8,128)(2,1)S(1)}, u32[]{:S(2)}, u32[]{:S(2)}) collective-permute-start(bf16[32,2176]{1,0:T(8,128)(2,1)S(1)} %get-tuple-element.29), channel_id=1, source_target_pairs={{0,2},{1,3},{2,0},{3,1},{4,6},{5,7},{6,4},{7,5},{8,10},{9,11},{10,... | collective-permute-start | bytes 417800 | tf_op jit(solution)/shard_map/ppermute | solution.py:405
  90.5 0.7 collective-permute-start.6
  91.2 0.0 collective-permute-done.4.refs_1_
  91.2 5.6 %collective-permute-done.5.refs_2_ = bf16[32,2176]{1,0:T(8,128)(2,1)S(1)} collective-permute-done((bf16[32,2176]{1,0:T(8,128)(2,1)S(1)}, bf16[32,2176]{1,0:T(8,128)(2,1)S(1)}, u32[]{:S(2)}, u32[]{:S(2)}) %collective-permute-start.5) | collective-permute-done | bytes 139296 | tf_op jit(solution)/shard_map/ppermute | solution.py:405
  96.8 3.0 %collective-permute-done.6.refs_3_ = bf16[32,2176]{1,0:T(8,128)(2,1)S(1)} collective-permute-done((bf16[32,2176]{1,0:T(8,128)(2,1)S(1)}, bf16[32,2176]{1,0:T(8,128)(2,1)S(1)}, u32[]{:S(2)}, u32[]{:S(2)}) %collective-permute-start.6) | collective-permute-done | bytes 139296 | tf_op jit(solution)/shard_map/ppermute | solution.py:405
  99.8 0.0 all-to-all-done.1.refs_4_
  99.8 1.6 %finish.1 = (f32[128,2048]{1,0:T(8,128)}, f32[16,128]{1,0:T(8,128)}, f32[16,128]{1,0:T(8,128)}) custom-call(s32[3]{0:T(128)S(1)} %copy-done.1, bf16[32,2176]{1,0:T(8,128)(2,1)S(1)} %get-tuple-element.27.refs_0_, bf16[32,2176]{1,0:T(8,128)(2,1)S(1)} %collective-permute-done.4.refs_1_, bf16[32,2176]{1,0:T(8,128)(2,1)S(1)} %collective-permute-done.5.refs_2_, ...), custom_call_target="tpu_custom_call" | custom-call | flops 1048576 | bytes 2097152 | tf_op jit(solution)/shard_map/finish/pallas_call | solution.py:386
  (1 shorter events, 0.0 us)
Async XLA Ops:
  0.6 36.1 %copy-start = (bf16[128,8192]{1,0:T(8,128)(2,1)S(1)}, bf16[128,8192]{1,0:T(8,128)(2,1)}, u32[]{:S(2)}) copy-start(bf16[128,8192]{1,0:T(8,128)(2,1)} %param.10) | copy-start | bytes 6291460
  1.6 34.1 %copy-start.6 = (f32[128]{0:T(128)S(1)}, f32[128]{0:T(128)}, u32[]{:S(2)}) copy-start(f32[128]{0:T(128)} %param.13) | copy-start | bytes 1540
  1.6 34.3 %copy-start.5 = (f32[128,64]{0,1:T(8,128)S(1)}, f32[128,64]{0,1:T(8,128)}, u32[]{:S(2)}) copy-start(f32[128,64]{0,1:T(8,128)} %param.11) | copy-start | bytes 98308
  32.0 5.8 %collective-permute-start = (bf16[1024,768]{1,0:T(8,128)(2,1)}, bf16[1024,768]{1,0:T(8,128)(2,1)}, u32[]{:S(2)}, u32[]{:S(2)}) collective-permute-start(bf16[1024,768]{1,0:T(8,128)(2,1)} %bitcast.5.own_hbm.own_ref), channel_id=1, source_target_pairs={{0,1},{1,0},{2,3},{3,2},{4,5},{5,4},{6,7},{7,6},{8,9},{9,8},{10,11... | collective-permute-start | bytes 4718600 | tf_op jit(solution)/shard_map/ppermute | solution.py:423
  36.8 28.0 %copy-start.1 = (s32[3]{0:T(128)S(1)}, s32[3]{0:T(128)}, u32[]{:S(2)}) copy-start(s32[3]{0:T(128)} %pad_add_fusion.where) | copy-start | bytes 40
  60.9 10.1 %collective-permute-start.1 = (bf16[32,2048]{1,0:T(8,128)(2,1)}, bf16[32,2048]{1,0:T(8,128)(2,1)S(1)}, u32[]{:S(2)}, u32[]{:S(2)}) collective-permute-start(bf16[32,2048]{1,0:T(8,128)(2,1)} %get-tuple-element.20), channel_id=1, source_target_pairs={{0,1},{1,0},{2,3},{3,2},{4,5},{5,4},{6,7},{7,6},{8,9},{9,8},{10,11... | collective-permute-start | bytes 393224 | tf_op jit(solution)/shard_map/ppermute | solution.py:405
  61.4 9.7 %collective-permute-start.2 = (bf16[32,2048]{1,0:T(8,128)(2,1)}, bf16[32,2048]{1,0:T(8,128)(2,1)S(1)}, u32[]{:S(2)}, u32[]{:S(2)}) collective-permute-start(bf16[32,2048]{1,0:T(8,128)(2,1)} %get-tuple-element.21), channel_id=1, source_target_pairs={{0,2},{1,3},{2,0},{3,1},{4,6},{5,7},{6,4},{7,5},{8,10},{9,11},{10,... | collective-permute-start | bytes 393224 | tf_op jit(solution)/shard_map/ppermute | solution.py:405
  64.7 7.3 %collective-permute-start.3 = (bf16[32,2048]{1,0:T(8,128)(2,1)}, bf16[32,2048]{1,0:T(8,128)(2,1)S(1)}, u32[]{:S(2)}, u32[]{:S(2)}) collective-permute-start(bf16[32,2048]{1,0:T(8,128)(2,1)} %get-tuple-element.22), channel_id=1, source_target_pairs={{0,3},{1,2},{2,1},{3,0},{4,7},{5,6},{6,5},{7,4},{8,11},{9,10},{10,... | collective-permute-start | bytes 393224 | tf_op jit(solution)/shard_map/ppermute | solution.py:405
  64.8 7.2 %copy-start.4 = (bf16[32,2048]{1,0:T(8,128)(2,1)S(1)}, bf16[32,2048]{1,0:T(8,128)(2,1)}, u32[]{:S(2)}) copy-start(bf16[32,2048]{1,0:T(8,128)(2,1)} %get-tuple-element.19.refs_0_) | copy-start | bytes 393220
  71.0 4.4 %copy-start.2 = (s32[64,2048]{1,0:T(8,128)}, s32[64,2048]{1,0:T(8,128)S(1)}, u32[]{:S(2)}) copy-start(s32[64,2048]{1,0:T(8,128)S(1)} %get-tuple-element.24.refs_6_.bits_ref) | copy-start | bytes 1572868
  75.4 24.4 %all-to-all-start.1 = ((bf16[128,16,128]{2,1,0:T(8,128)(2,1)}), bf16[128,16,128]{2,1,0:T(8,128)(2,1)S(1)}, u32[]{:S(2)}, u32[]{:S(2)}) async-start(bf16[128,16,128]{2,1,0:T(8,128)(2,1)} %bitcast.9), calls=%async_computation.1 | async-start | bytes 1048576 | tf_op jit(solution)/shard_map/all_to_all | solution.py:434
  81.3 1.0 %copy-start.3 = (s32[64,2048]{1,0:T(8,128)S(1)}, s32[64,2048]{1,0:T(8,128)}, u32[]{:S(2)}) copy-start(s32[64,2048]{1,0:T(8,128)} %copy-done.2) | copy-start | bytes 1572868
  86.8 4.4 %collective-permute-start.4 = (bf16[32,2176]{1,0:T(8,128)(2,1)S(1)}, bf16[32,2176]{1,0:T(8,128)(2,1)S(1)}, u32[]{:S(2)}, u32[]{:S(2)}) collective-permute-start(bf16[32,2176]{1,0:T(8,128)(2,1)S(1)} %get-tuple-element.28), channel_id=1, source_target_pairs={{0,1},{1,0},{2,3},{3,2},{4,5},{5,4},{6,7},{7,6},{8,9},{9,8},{10,11... | collective-permute-start | bytes 417800 | tf_op jit(solution)/shard_map/ppermute | solution.py:405
  88.0 8.8 %collective-permute-start.5 = (bf16[32,2176]{1,0:T(8,128)(2,1)S(1)}, bf16[32,2176]{1,0:T(8,128)(2,1)S(1)}, u32[]{:S(2)}, u32[]{:S(2)}) collective-permute-start(bf16[32,2176]{1,0:T(8,128)(2,1)S(1)} %get-tuple-element.29), channel_id=1, source_target_pairs={{0,2},{1,3},{2,0},{3,1},{4,6},{5,7},{6,4},{7,5},{8,10},{9,11},{10,... | collective-permute-start | bytes 417800 | tf_op jit(solution)/shard_map/ppermute | solution.py:405
  90.5 9.2 %collective-permute-start.6 = (bf16[32,2176]{1,0:T(8,128)(2,1)S(1)}, bf16[32,2176]{1,0:T(8,128)(2,1)S(1)}, u32[]{:S(2)}, u32[]{:S(2)}) collective-permute-start(bf16[32,2176]{1,0:T(8,128)(2,1)S(1)} %get-tuple-element.30), channel_id=1, source_target_pairs={{0,3},{1,2},{2,1},{3,0},{4,7},{5,6},{6,5},{7,4},{8,11},{9,10},{10,... | collective-permute-start | bytes 417800 | tf_op jit(solution)/shard_map/ppermute | solution.py:405
